TPU v7x, 256 devices: a whole 4x4x8 slice. The times are simulated.
256 devices in a mesh: grp: 2 (over core), cell: 128 (over y, x, z).
Axes of the slice: x: 4, y: 4, z: 8, core: 2. Of those that a mesh axis runs over, the one named last changes fastest.
Arguments:
- path_delay: float32 [1064960], P('cell'), may hold values from 0 to 64
- path_angle: float32 [1064960], P('cell'), may hold values from -3.140625 to 3.140625
- path_gain: float32 [2, 1064960], P(None, 'cell'), may hold values from -0.9 to 0.9
- slot_counts: int32 [32768], P('cell'), may hold values from 1 to 64, as said below
- slot_offsets: int32 [32768], P('cell'), may hold values from 0 to 8319, as said below
- ray_link: int32 [32768], P('cell'), may hold values from 0 to 32767, as said below
- nearby_sectors: int32 [8, 4096], P(None, 'cell'), may hold values from 0 to 4095, as said below
- serving_slot: int32 [4096], P('cell'), may hold values from 0 to 7
- symbols: bfloat16 [4096, 2, 128], P('cell'), may hold values from -4 to 4
Outputs:
- received: float32 [4096, 2, 128], P('cell')
Inputs may be any that keep to these rules, and one draw needn't show every extreme that they name: `slot_counts`: the counts of one device's 256 ray slots sum to 8320, and every device has a slot of 64 paths. The ray slots of one device hold at most 130 paths of links of one owner, and exactly 130 for some owner. Within one device, the ranges slot_offsets to slot_offsets + slot_counts - 1 of its 256 slots cover the device's 8320 paths once each. `ray_link`: every link appears in exactly one ray slot. The owner of link g is the device g // 256, which holds its user; within the ray slots of one device the owners never fall. The ray slots of one device hold at most 4 links of one owner, and exactly 4 of some owner; every owner has 256 links in all. `nearby_sectors`: entry serving_slot[u] of user u is its serving sector, one of the sectors of the device that holds the user; every other entry lies within 16 sector indices of the serving sector, and on every device some user has entries at distance exactly 16.
All inputs are finite; a program needn't handle non-finite values.
Results may differ from a plain program's by a relative error of at most 0.0027.
Values may be sent and summed in bfloat16 or wider, within the bound.
A program may use at most 64 MiB of HBM per device.

v0:
```python
import math

import jax
import jax.numpy as jnp
from jax import lax
from jax.sharding import PartitionSpec as P

SECTOR_ANTENNAS = 64
FRAME_TONES = 128
PMAX = 64
NEARBY_COUNT = 8
CELL_SECTORS = 32
REACH = 16


EPSILON = 1e-06
FINE_STEPS = 16


def joined_along(parts, dim):
    lengths = list(parts.shape[1:])
    lengths[dim] *= parts.shape[0]
    return jnp.moveaxis(parts, 0, dim).reshape(lengths)


def copy_for_each(x, axis):
    copies = jnp.broadcast_to(x, (lax.axis_size(axis), *x.shape))
    return lax.all_to_all(copies, axis, split_axis=0, concat_axis=0, tiled=True)


def gathered_copies(x, axis, dim):
    return joined_along(copy_for_each(x, axis), dim)


def extended(x, sides, width):
    for axis, dim in sides:
        size, length = (lax.axis_size(axis), x.shape[dim])
        up = [(i, (i + 1) % size) for i in range(size - 1)]
        down = [(j, i) for i, j in up]
        last = lax.slice_in_dim(x, length - width, length, axis=dim)
        initial = lax.slice_in_dim(x, 0, width, axis=dim)
        before = lax.ppermute(last, axis, up)
        after = lax.ppermute(initial, axis, down)
        x = jnp.concatenate([before, x, after], axis=dim)
    return x


def taken_together(x, axis):
    return copy_for_each(x, axis).sum(axis=0)


def delay_table(delay_rows):
    coarse_count = FRAME_TONES // FINE_STEPS
    coarse_freq = (
        jnp.arange(coarse_count, dtype=jnp.float32) * FINE_STEPS - FRAME_TONES // 2
    ) / FRAME_TONES
    fine_freq = jnp.arange(FINE_STEPS, dtype=jnp.float32) / FRAME_TONES
    coarse_phase = 2 * math.pi * delay_rows[:, :, None] * coarse_freq[None, None, :]
    fine_phase = 2 * math.pi * delay_rows[:, :, None] * fine_freq[None, None, :]
    coarse_cos = jnp.cos(coarse_phase)[:, :, :, None]
    coarse_sin = jnp.sin(coarse_phase)[:, :, :, None]
    fine_cos = jnp.cos(fine_phase)[:, :, None, :]
    fine_sin = jnp.sin(fine_phase)[:, :, None, :]
    shape_out = (delay_rows.shape[0], delay_rows.shape[1], FRAME_TONES)
    delay_real = (coarse_cos * fine_cos - coarse_sin * fine_sin).reshape(shape_out)
    delay_imag = (-(coarse_sin * fine_cos + coarse_cos * fine_sin)).reshape(shape_out)
    return jnp.concatenate([delay_real, delay_imag], axis=1).astype(jnp.bfloat16)


def make_response(delay_rows, angle_rows, real_rows, imag_rows, antenna_array):
    delay_stack = delay_table(delay_rows)
    steer_phase = math.pi * antenna_array[None, :, None] * jnp.sin(angle_rows)[:, None, :]
    steer_cos = jnp.cos(steer_phase)
    steer_sin = jnp.sin(steer_phase)
    spread_real = (real_rows[:, None, :] * steer_cos + imag_rows[:, None, :] * steer_sin).astype(
        jnp.bfloat16
    )
    spread_imag = (imag_rows[:, None, :] * steer_cos - real_rows[:, None, :] * steer_sin).astype(
        jnp.bfloat16
    )
    upper = jnp.concatenate([spread_real, -spread_imag], axis=2)
    lower = jnp.concatenate([spread_imag, spread_real], axis=2)
    mixing = jnp.concatenate([upper, lower], axis=1)
    response = jnp.einsum("bap,bpf->baf", mixing, delay_stack, preferred_element_type=jnp.float32)
    return response.astype(jnp.bfloat16).reshape(
        delay_rows.shape[0], 2, antenna_array.shape[0], FRAME_TONES
    )


def link_signal(response, padded, sector_local):
    remote = padded[sector_local]
    resp_real = response[:, 0]
    resp_imag = response[:, 1]
    remote_real = remote[:, 0]
    remote_imag = remote[:, 1]

    def product(left, right):
        return jnp.einsum("baf,baf->bf", left, right, preferred_element_type=jnp.float32)

    recv_real = product(resp_real, remote_real) - product(resp_imag, remote_imag)
    recv_imag = product(resp_real, remote_imag) + product(resp_imag, remote_real)
    return jnp.stack([recv_real, recv_imag], axis=1)


def shards(
    path_delay,
    path_angle,
    path_gain,
    slot_counts,
    slot_offsets,
    ray_link,
    nearby_sectors,
    serving_slot,
    symbols,
):
    devices = lax.axis_size("cell")
    here = lax.axis_index("cell")
    worker_count = lax.axis_size("grp")
    worker_index = lax.axis_index("grp")
    path_total = path_delay.shape[0]
    link_total = slot_counts.shape[0]
    total_users = serving_slot.shape[0]
    capacity = 2 * link_total // devices
    owner_grid = jnp.arange(devices, dtype=jnp.int32)
    owner_of = ray_link // link_total
    bucket_size = jnp.sum((owner_of[:, None] == owner_grid[None, :]).astype(jnp.int32), axis=0)
    bucket_start = jnp.cumsum(bucket_size) - bucket_size
    slot_grid = jnp.arange(capacity, dtype=jnp.int32)
    send_live = slot_grid[None, :] < bucket_size[:, None]
    send_slot = jnp.where(send_live, bucket_start[:, None] + slot_grid[None, :], 0).reshape(
        devices * capacity
    )
    send_live = send_live.reshape(devices * capacity)
    local_link = jnp.where(
        send_live, ray_link[send_slot] - jnp.repeat(owner_grid, capacity) * link_total, -1
    )
    link_tags = local_link.astype(jnp.float32)[None, :]
    send_counts = jnp.where(send_live, slot_counts[send_slot], 0)
    send_first = slot_offsets[send_slot]
    path_width = PMAX // worker_count
    path_begin = worker_index * path_width
    path_steps = path_begin + jnp.arange(path_width, dtype=jnp.int32)
    live_mask = send_live[:, None] & (path_steps[None, :] < send_counts[:, None])
    where_path = jnp.clip(send_first[:, None] + path_steps[None, :], 0, path_total - 1)
    columns = (path_delay, path_angle, path_gain[0], path_gain[1])
    packed = jnp.stack([jnp.where(live_mask, column[where_path], 0.0) for column in columns])
    arrived, arrived_tags = (
        lax.all_to_all(packed, "cell", split_axis=1, concat_axis=1, tiled=True),
        lax.all_to_all(link_tags, "cell", split_axis=1, concat_axis=1, tiled=True),
    )
    arrived = gathered_copies(arrived, "grp", 2)
    target = arrived_tags[0].astype(jnp.int32)
    target = jnp.where(target >= 0, target, link_total)
    placed = (
        jnp.zeros((4, link_total, PMAX), jnp.float32).at[:, target, :].set(arrived, mode="drop")
    )
    antenna_portion = SECTOR_ANTENNAS // worker_count
    antenna_array = (
        worker_index * antenna_portion + jnp.arange(antenna_portion, dtype=jnp.int32)
    ).astype(jnp.float32)

    def respond(link_rows):
        return make_response(link_rows[0], link_rows[1], link_rows[2], link_rows[3], antenna_array)

    user_grid = jnp.arange(total_users, dtype=jnp.int32)
    serve_links = user_grid * NEARBY_COUNT + serving_slot
    serve_sector = (
        jnp.take_along_axis(nearby_sectors, serving_slot[None, :], axis=0)[0] - here * CELL_SECTORS
    )
    nearby_local = nearby_sectors - here * CELL_SECTORS + REACH
    user_block = 16
    block_count = total_users // user_block
    link_index = jnp.arange(link_total, dtype=jnp.int32)

    def one_block(block_id):
        chosen = lax.dynamic_slice_in_dim(
            link_index, block_id * user_block * NEARBY_COUNT, user_block * NEARBY_COUNT
        )
        return respond(placed[:, chosen, :])

    final_output = lax.map(one_block, jnp.arange(block_count, dtype=jnp.int32))
    channel_responses = final_output.reshape(
        total_users * NEARBY_COUNT, 2, antenna_portion, FRAME_TONES
    )
    serving_response = channel_responses[serve_links]
    symbol_rows = symbols.astype(jnp.float32)
    resp_real = serving_response[:, 0].astype(jnp.float32)
    resp_imag = serving_response[:, 1].astype(jnp.float32)
    contribution_real = (
        resp_real * symbol_rows[:, 0, None, :] + resp_imag * symbol_rows[:, 1, None, :]
    )
    contribution_imag = (
        resp_real * symbol_rows[:, 1, None, :] - resp_imag * symbol_rows[:, 0, None, :]
    )
    path_contribution = jnp.stack([contribution_real, contribution_imag], axis=1).reshape(
        total_users, 2 * antenna_portion * FRAME_TONES
    )
    selector = (jnp.arange(CELL_SECTORS, dtype=jnp.int32)[:, None] == serve_sector[None, :]).astype(
        jnp.float32
    )
    unscaled_signal = jnp.dot(
        selector,
        path_contribution,
        precision=lax.Precision.HIGHEST,
        preferred_element_type=jnp.float32,
    )
    unscaled_signal = unscaled_signal.reshape(CELL_SECTORS, 2, antenna_portion, FRAME_TONES)
    antenna_power = jnp.mean(
        unscaled_signal[:, 0] * unscaled_signal[:, 0]
        + unscaled_signal[:, 1] * unscaled_signal[:, 1],
        axis=2,
    )
    transmit_weights = (
        unscaled_signal / jnp.sqrt(antenna_power + EPSILON)[:, None, :, None]
    ).astype(jnp.bfloat16)
    padded = extended(transmit_weights, (("cell", 0),), REACH)
    every_part = link_signal(channel_responses, padded, nearby_local.T.reshape(link_total))
    partial_value = jnp.sum(every_part.reshape(total_users, NEARBY_COUNT, 2, FRAME_TONES), axis=1)
    summed_signal = taken_together(partial_value, "grp")
    return summed_signal / math.sqrt(SECTOR_ANTENNAS)


def solution(mesh):
    placed = (
        P("cell"),
        P("cell"),
        P(None, "cell"),
        P("cell"),
        P("cell"),
        P("cell"),
        P(None, "cell"),
        P("cell"),
        P("cell", None, None),
    )
    return jax.shard_map(
        shards, mesh=mesh, in_specs=placed, out_specs=P("cell", None, None), check_vma=False
    )
```

profile of v0, /device:TPU:1, one launch (start us, length us, event | category | flops | bytes accessed | tf_op | source)
XLA Modules:
  0.0 558.4 jit_solution(14054159414212339889)
XLA Ops:
  0.0 0.7 and_select_fusion.1
  1.5 3.6 gather_fusion.1
  5.3 0.8 copy.59
  6.1 16.9 %all-to-all-start = ((f32[1,128,4]{2,0,1:T(1,128)}), f32[1,128,4]{2,0,1:T(1,128)}, u32[]{:S(2)}, u32[]{:S(2)}) async-start(f32[1,128,4]{2,0,1:T(1,128)} %copy.59), calls=%async_computation | async-start | bytes 131072 | tf_op jit(solution)/shard_map/all_to_all | solution.py:149
  22.9 0.7 iota_compare_fusion.1
  23.6 3.5 gather_fusion.3
  27.2 0.5 copy-done.13
  28.2 90.5 %gather_fusion.6 = f32[16384]{0:T(1024)S(1)} fusion(f32[8320]{0:T(1024)S(1)} %get-tuple-element.109, s32[16384]{0:T(1024)S(1)} %broadcast_clamp_fusion), kind=kCustom, calls=%fused_computation.6 | custom fusion | bytes 196608 | tf_op jit(solution)/shard_map/gather | solution.py:146
  118.7 0.8 gather.58
  119.5 90.5 %gather_fusion.7 = f32[16384]{0:T(1024)S(1)} fusion(f32[8320]{0:T(1024)S(1)} %get-tuple-element.110, s32[16384]{0:T(1024)S(1)} %broadcast_clamp_fusion), kind=kCustom, calls=%fused_computation.7 | custom fusion | bytes 196608 | tf_op jit(solution)/shard_map/gather | solution.py:146
  210.1 0.8 gather.60
  210.9 90.5 %gather_fusion.4 = f32[16384]{0:T(1024)S(1)} fusion(f32[8320]{0:T(1024)S(1)} %copy-done, s32[16384]{0:T(1024)S(1)} %broadcast_clamp_fusion), kind=kCustom, calls=%fused_computation.4 | custom fusion | bytes 196608 | tf_op jit(solution)/shard_map/gather | solution.py:146
  301.5 0.6 copy-done.1
  302.2 90.5 %gather_fusion.5 = f32[16384]{0:T(1024)S(1)} fusion(f32[8320]{0:T(1024)S(1)} %copy-done.1, s32[16384]{0:T(1024)S(1)} %broadcast_clamp_fusion), kind=kCustom, calls=%fused_computation.5 | custom fusion | bytes 196608 | tf_op jit(solution)/shard_map/gather | solution.py:146
  392.9 3.5 gather_fusion.2
  396.7 0.7 gather_fusion.10
  397.7 0.7 copy.104
  398.4 1.4 reshape.819
  399.9 13.4 %all-to-all-start.1 = ((f32[128,1,512]{2,1,0:T(1,128)}), f32[128,1,512]{2,1,0:T(1,128)S(1)}, u32[]{:S(2)}, u32[]{:S(2)}) async-start(f32[128,1,512]{2,1,0:T(1,128)} %reshape.819), calls=%async_computation.1 | async-start | bytes 524288 | tf_op jit(solution)/shard_map/all_to_all | solution.py:148
  413.4 1.0 convert_reduce_fusion.1
  414.5 11.6 %all-to-all-done.1 = f32[128,1,512]{2,1,0:T(1,128)S(1)} async-done(((f32[128,1,512]{2,1,0:T(1,128)}), f32[128,1,512]{2,1,0:T(1,128)S(1)}, u32[]{:S(2)}, u32[]{:S(2)}) %all-to-all-start.1) | async-done | bytes 262176 | tf_op jit(solution)/shard_map/all_to_all | solution.py:148
  426.2 0.5 broadcast.673
  426.7 1.2 reduce.18
  427.9 0.5 reshape.820
  428.9 6.8 %all_to_all.21 = f32[2,4,512,32]{2,3,1,0:T(8,128)S(1)} all-to-all(f32[2,4,512,32]{2,3,1,0:T(8,128)S(1)} %broadcast_in_dim.96), channel_id=1, replica_groups=mesh['grp'=2,'cell'=128] {'grp'}, dimensions={0} | all-to-all | bytes 1048576 | tf_op jit(solution)/shard_map/all_to_all | solution.py:28
  435.7 0.4 copy.63
  436.2 14.2 %scatter_fusion = f32[4,256,64]{2,0,1:T(4,128)S(1)} fusion(f32[4,256,64]{2,0,1:T(4,128)S(1)} %broadcast_in_dim.89, s32[512]{0:T(512)S(1)} %bitcast.135, f32[512,4,64]{2,1,0:T(4,128)S(1)} %copy.63), kind=kCustom, calls=%fused_computation.11 | custom fusion | bytes 1574912 | tf_op jit(solution)/shard_map/scatter | solution.py:155
  450.4 74.6 %while.13 = (s32[]{:T(128)}, bf16[2,128,2,32,128]{4,3,2,1,0:T(8,128)(2,1)}, s32[2]{0:T(128)S(1)}, s32[256]{0:T(256)S(1)}, f32[4,256,64]{2,0,1:T(4,128)S(1)}, /*i...) while((s32[]{:T(128)}, bf16[2,128,2,32,128]{4,3,2,1,0:T(8,128)(2,1)}, ...), condition=%wide.region_4.5_spmd.clone, body=%wide.region_3.4_spmd.clone.sunk | while | flops 300361216 | bytes 38608128 | solution.py:181
  450.4 0.6 dynamic_slice.19
  451.7 0.7 gather_fusion
  452.5 1.8 fusion.58
  454.4 1.9 multiply_cosine_fusion.5
  456.4 1.0 multiply_cosine_fusion.6
  457.3 2.6 subtract_convert_fusion.2
  460.0 4.2 copy.109
  464.1 2.8 copy.110
  467.0 8.1 %fusion.59 = (bf16[128,32,64]{2,1,0:T(8,128)(2,1)S(1)}, bf16[128,32,64]{2,1,0:T(8,128)(2,1)S(1)}) fusion(f32[128,64]{1,0:T(8,128)S(1)} %bitcast.121, f32[128,64]{1,0:T(8,128)S(1)} %bitcast.123, f32[32]{0:T(128)S(1)} %convert_multiply_fusion.10, f32[128,64]{1,0:T(8,128)S(1)} %bitcast.119), kind=kLoop, calls=%fused_computation.28.clone.2 | loop fusion | flops 2359296 | bytes 1147008 | tf_op jit(solution)/shard_map/while/body/eval_jaxpr/convert_element_type | solution.py:78
  475.1 7.9 %fusion.60 = bf16[128,32,64]{2,1,0:T(8,128)(2,1)S(1)} fusion(f32[128,64]{1,0:T(8,128)S(1)} %bitcast.120, f32[128,64]{1,0:T(8,128)S(1)} %bitcast.124, f32[32]{0:T(128)S(1)} %convert_multiply_fusion.10, f32[128,64]{1,0:T(8,128)S(1)} %bitcast.122), kind=kLoop, calls=%fused_computation.50.clone.1 | loop fusion | flops 2097152 | bytes 622720 | tf_op jit(solution)/shard_map/while/body/eval_jaxpr/neg | solution.py:81
  483.0 2.9 fusion.61
  486.0 1.8 constant_dynamic-update-slice_fusion.2
  487.8 0.6 dynamic_slice.19
  489.1 0.7 gather_fusion
  489.8 1.8 fusion.58
  491.8 1.9 multiply_cosine_fusion.5
  493.7 1.0 multiply_cosine_fusion.6
  494.7 2.6 subtract_convert_fusion.2
  497.3 4.2 copy.109
  501.5 2.8 copy.110
  504.3 8.1 %fusion.59 = (bf16[128,32,64]{2,1,0:T(8,128)(2,1)S(1)}, bf16[128,32,64]{2,1,0:T(8,128)(2,1)S(1)}) fusion(f32[128,64]{1,0:T(8,128)S(1)} %bitcast.121, f32[128,64]{1,0:T(8,128)S(1)} %bitcast.123, f32[32]{0:T(128)S(1)} %convert_multiply_fusion.10, f32[128,64]{1,0:T(8,128)S(1)} %bitcast.119), kind=kLoop, calls=%fused_computation.28.clone.2 | loop fusion | flops 2359296 | bytes 1147008 | tf_op jit(solution)/shard_map/while/body/eval_jaxpr/convert_element_type | solution.py:78
  512.4 7.9 %fusion.60 = bf16[128,32,64]{2,1,0:T(8,128)(2,1)S(1)} fusion(f32[128,64]{1,0:T(8,128)S(1)} %bitcast.120, f32[128,64]{1,0:T(8,128)S(1)} %bitcast.124, f32[32]{0:T(128)S(1)} %convert_multiply_fusion.10, f32[128,64]{1,0:T(8,128)S(1)} %bitcast.122), kind=kLoop, calls=%fused_computation.50.clone.1 | loop fusion | flops 2097152 | bytes 622720 | tf_op jit(solution)/shard_map/while/body/eval_jaxpr/neg | solution.py:81
  520.4 2.9 fusion.61
  523.3 1.7 constant_dynamic-update-slice_fusion.2
  525.0 2.8 gather_fusion.8
  528.1 0.6 copy.103
  528.9 1.3 fusion.32
  530.7 2.2 collective-permute-start
  532.9 1.3 collective-permute-start.1
  534.3 4.0 collective-permute-done
  538.2 3.8 collective-permute-done.1
  542.1 0.7 copy.66
  542.8 3.1 gather_fusion.9
  545.9 6.8 %fusion.30 = (f32[256,128]{1,0:T(8,128)S(1)}, f32[256,128]{1,0:T(8,128)S(1)}, f32[256,128]{1,0:T(8,128)S(1)}, f32[256,128]{1,0:T(8,128)S(1)}) fusion(bf16[256,2,32,128]{3,2,1,0:T(8,128)(2,1)} %bitcast.14, bf16[256,2,32,128]{3,2,1,0:T(8,128)(2,1)} %gather_fusion.9), kind=kLoop, calls=%fused_computation.57 | loop fusion | flops 12451840 | bytes 8912896 | tf_op jit(solution)/shard_map/baf,baf->bf/dot_general | solution.py:98
  552.8 5.0 all_to_all.22
  557.8 0.6 copy.67
  (102 shorter events, 4.4 us)
Async XLA Ops:
  0.0 210.9 %copy-start = (f32[8320]{0:T(1024)S(1)}, f32[8320]{0:T(1024)}, u32[]{:S(2)}) copy-start(f32[8320]{0:T(1024)} %param.11) | copy-start | bytes 99844
  0.0 23.6 %copy-start.2 = (s32[256]{0:T(256)S(1)}, s32[256]{0:T(256)}, u32[]{:S(2)}) copy-start(s32[256]{0:T(256)} %param.15) | copy-start | bytes 3076
  1.5 25.7 %copy-start.11 = (s32[1024]{0:T(1024)}, s32[1024]{0:T(1024)S(1)}, u32[]{:S(2)}) copy-start(s32[1024]{0:T(1024)S(1)} %pad_clamp_fusion.3) | copy-start | bytes 12292
  5.1 22.9 %copy-start.8 = (f32[2,8320]{1,0:T(2,128)S(1)}, f32[2,8320]{1,0:T(2,128)}, u32[]{:S(2)}) copy-start(f32[2,8320]{1,0:T(2,128)} %param.13) | copy-start | bytes 199684
  6.1 393.9 %all-to-all-start = ((f32[1,128,4]{2,0,1:T(1,128)}), f32[1,128,4]{2,0,1:T(1,128)}, u32[]{:S(2)}, u32[]{:S(2)}) async-start(f32[1,128,4]{2,0,1:T(1,128)} %copy.59), calls=%async_computation | async-start | bytes 131072 | tf_op jit(solution)/shard_map/all_to_all | solution.py:149
  27.2 0.5 copy-start.13
  301.4 0.8 copy-start.1
  302.2 90.7 %copy-start.3 = (s32[256]{0:T(256)S(1)}, s32[256]{0:T(256)}, u32[]{:S(2)}) copy-start(s32[256]{0:T(256)} %param.14) | copy-start | bytes 3076
  302.2 90.7 %copy-start.12 = (s32[1024]{0:T(1024)S(1)}, s32[1024]{0:T(1024)}, u32[]{:S(2)}) copy-start(s32[1024]{0:T(1024)} %copy-done.11) | copy-start | bytes 12292
  392.7 3.7 copy-start.10
  392.7 3.9 copy-start.15
  392.7 3.9 copy-start.4
  392.8 4.6 copy-start.6
  392.8 4.6 copy-start.7
  392.8 4.6 copy-start.14
  397.7 15.6 %copy-start.9 = (bf16[32,2,128]{2,1,0:T(2,128)(2,1)S(1)}, bf16[32,2,128]{2,1,0:T(2,128)(2,1)}, u32[]{:S(2)}) copy-start(bf16[32,2,128]{2,1,0:T(2,128)(2,1)} %param.19) | copy-start | bytes 49156
  399.9 26.2 %all-to-all-start.1 = ((f32[128,1,512]{2,1,0:T(1,128)}), f32[128,1,512]{2,1,0:T(1,128)S(1)}, u32[]{:S(2)}, u32[]{:S(2)}) async-start(f32[128,1,512]{2,1,0:T(1,128)} %reshape.819), calls=%async_computation.1 | async-start | bytes 524288 | tf_op jit(solution)/shard_map/all_to_all | solution.py:148
  467.0 16.1 %copy-start.5 = (bf16[128,64,128]{2,1,0:T(8,128)(2,1)S(1)}, bf16[128,64,128]{2,1,0:T(8,128)(2,1)}, u32[]{:S(2)}) copy-start(bf16[128,64,128]{2,1,0:T(8,128)(2,1)} %copy.109) | copy-start | bytes 6291460 | tf_op jit(solution)/shard_map/while
  504.3 16.1 %copy-start.5 = (bf16[128,64,128]{2,1,0:T(8,128)(2,1)S(1)}, bf16[128,64,128]{2,1,0:T(8,128)(2,1)}, u32[]{:S(2)}) copy-start(bf16[128,64,128]{2,1,0:T(8,128)(2,1)} %copy.109) | copy-start | bytes 6291460 | tf_op jit(solution)/shard_map/while
  530.7 7.5 %collective-permute-start = (bf16[16,2,32,128]{3,0,2,1:T(8,128)(2,1)S(1)}, bf16[16,2,32,128]{3,0,2,1:T(8,128)(2,1)S(1)}, u32[]{:S(2)}, u32[]{:S(2)}) collective-permute-start(bf16[16,2,32,128]{3,0,2,1:T(8,128)(2,1)S(1)} %get-tuple-element.137), channel_id=1, source_target_pairs={{0,1},{1,2},{2,3},{3,4},{4,5},{5,6},{6,7},{7,8},{8,9},{9,10},{10,1... | collective-permute-start | bytes 786440 | tf_op jit(solution)/shard_map/ppermute | solution.py:42
  532.9 9.1 %collective-permute-start.1 = (bf16[16,2,32,128]{3,0,2,1:T(8,128)(2,1)S(1)}, bf16[16,2,32,128]{3,0,2,1:T(8,128)(2,1)S(1)}, u32[]{:S(2)}, u32[]{:S(2)}) collective-permute-start(bf16[16,2,32,128]{3,0,2,1:T(8,128)(2,1)S(1)} %get-tuple-element.138), channel_id=1, source_target_pairs={{1,0},{2,1},{3,2},{4,3},{5,4},{6,5},{7,6},{8,7},{9,8},{10,9},{11,1... | collective-permute-start | bytes 786440 | tf_op jit(solution)/shard_map/ppermute | solution.py:43
where the time goes:
time: 559 us; the launch traced here: 558 us
  local copies, waits for them, and re-layouts  425 us (76%)
  other arithmetic  59.4 us (11%)
  starting transfers between devices  33.7 us (6%)
  waiting for transfers between devices  19.4 us (3%)
  blocking collectives  11.8 us (2%)
  matrix products  7.12 us (1%)
    gather x8, local copies, waits for them, and re-layouts, shards(): column[where_path]  364 us
    all_to_all x1, starting transfers between devices, shards(): lax.all_to_all(link_tags, 'cell', split_axis=1, concat_axis=1, tiled=True)  16.9 us
    convert_element_type x2, other arithmetic, make_response(): (imag_rows[:, None, :] * steer_cos - real_rows[:, None, :] * steer_sin).a...  16.2 us
    neg x2, other arithmetic, make_response(): upper = jnp.concatenate([spread_real, -spread_imag], axis=2)  15.8 us
    scatter x1, local copies, waits for them, and re-layouts, shards(): jnp.zeros((4, link_total, PMAX), jnp.float32).at[:, target, :]  14.2 us
    all_to_all x1, starting transfers between devices, shards(): lax.all_to_all(packed, 'cell', split_axis=1, concat_axis=1, tiled=True)  13.4 us
    all_to_all x2, blocking collectives, copy_for_each(): return lax.all_to_all(copies, axis, split_axis=0, concat_axis=0, tiled=True)  11.8 us
    all_to_all x1, waiting for transfers between devices, shards(): lax.all_to_all(packed, 'cell', split_axis=1, concat_axis=1, tiled=True)  11.6 us
  transfers between devices with their start and end apart: 4, of which 3 were waited for; matrix products, arithmetic and copies ran while one was open for 67% of the time, Pallas kernels for 0%

commit v1 on v0

v1 whole, which is shorter than its diff:
```python
import functools
import math

import jax
import jax.numpy as jnp
from jax import lax
from jax.experimental import pallas as pl
from jax.experimental.pallas import tpu as pltpu
from jax.sharding import PartitionSpec as P

SECTOR_ANTENNAS = 64
FRAME_TONES = 128
NEARBY_COUNT = 8
CELL_SECTORS = 32
REACH = 16
EPSILON = 1e-06

CELLS = 128
SLOTS = 256
USERS = 32
LINKS = USERS * NEARBY_COUNT
PATH_ROWS = 65
ANT = SECTOR_ANTENNAS // 2
RESP = 2 * ANT
TAG_LANE = 8
VMEM_LIMIT = 48 * 1024 * 1024
MESH = pl.DeviceIdType.MESH


def lanes(shape):
    return lax.broadcasted_iota(jnp.int32, shape, len(shape) - 1)


def rows_of(shape):
    return lax.broadcasted_iota(jnp.int32, shape, len(shape) - 2)


def sincos_turns(turns):
    r = turns - jnp.round(turns)
    r2 = r * r
    sin_c = [(-1) ** n * math.pi ** (2 * n + 1) / math.factorial(2 * n + 1) for n in range(7)]
    cos_c = [(-1) ** n * math.pi ** (2 * n) / math.factorial(2 * n) for n in range(7)]
    sh = jnp.full_like(r, sin_c[-1])
    ch = jnp.full_like(r, cos_c[-1])
    for n in range(5, -1, -1):
        sh = sh * r2 + sin_c[n]
        ch = ch * r2 + cos_c[n]
    sh = sh * r
    return 2.0 * sh * ch, 1.0 - 2.0 * sh * sh


def pack_kernel(counts, offsets, links, delay, angle, gain, out, store):
    for c in range(0, PATH_ROWS, 8):
        n = min(8, PATH_ROWS - c)
        for f, ref in ((0, delay), (1, angle)):
            value = ref[c : c + n, :]
            value = value * (1.0 / FRAME_TONES) if f == 0 else jnp.sin(value)
            store[pl.ds(8 * (c + 1) + f, n, stride=8), :] = value
            store[pl.ds(8 * c + 4 + f, n, stride=8), :] = value
    for q in range(PATH_ROWS):
        pair = gain[:, 128 * q : 128 * (q + 1)]
        store[8 * (q + 1) + 2 : 8 * (q + 1) + 4, :] = pair
        store[8 * q + 6 : 8 * q + 8, :] = pair

    def clear(i, carry):
        out[pl.ds(pl.multiple_of(64 * i, 64), 64), :] = jnp.zeros((64, 128), jnp.float32)
        return carry

    lax.fori_loop(0, CELLS * 8 // 64, clear, 0)
    lane = lanes((8, 128))
    row = rows_of((8, 128))
    high = row >= 4
    place = lane + jnp.where(high, 128, 0)
    tag_place = jnp.where(row == 4, lane - TAG_LANE, -1000)

    def one(r, carry):
        before, k, base, last = carry
        link = links[r]
        owner = link >> 8
        same = owner == before
        k = jnp.where(same, k + 1, 0)
        base = jnp.where(same, base + last, 0)
        off = offsets[r]
        cnt = counts[r]
        q = off >> 7
        s = off & 127
        block = store[pl.ds(pl.multiple_of(8 * q + 8, 8), 8), :]
        turned = pltpu.roll(block, (base - s) & 127, 1)
        swapped = pltpu.roll(turned, 4, 0)
        j = place - base
        second = (j + s) >= 128
        value = jnp.where(second == high, turned, swapped)
        at = pl.ds(pl.multiple_of(8 * owner, 8), 8)
        new = jnp.where((j >= 0) & (j < cnt), value, out[at, :])
        new = jnp.where(tag_place == 2 * k, ((link & 255) + 1).astype(jnp.float32), new)
        new = jnp.where(tag_place == 2 * k + 1, cnt.astype(jnp.float32), new)
        out[at, :] = new
        return owner, k, base, cnt

    zero = jnp.int32(0)
    lax.fori_loop(0, SLOTS, one, (jnp.int32(-1), zero, zero, zero), unroll=8)


def exchange_kernel(sent, got, send_sem, recv_sem):
    me = lax.axis_index("cell")
    barrier = pltpu.get_barrier_semaphore()

    def greet(d, carry):
        other = lax.rem(me + d, CELLS)
        pl.semaphore_signal(barrier, inc=1, device_id={"cell": other}, device_id_type=MESH)
        return carry

    lax.fori_loop(1, CELLS, greet, 0)
    mine = pl.ds(pl.multiple_of(8 * me, 8), 8)
    got[mine, :] = sent[mine, :]
    pl.semaphore_wait(barrier, CELLS - 1)

    def send(d, carry):
        other = lax.rem(me + d, CELLS)
        pltpu.make_async_remote_copy(
            src_ref=sent.at[pl.ds(pl.multiple_of(8 * other, 8), 8), :],
            dst_ref=got.at[mine, :],
            send_sem=send_sem,
            recv_sem=recv_sem,
            device_id={"cell": other},
            device_id_type=MESH,
        ).start()
        return carry

    lax.fori_loop(1, CELLS, send, 0)
    rest = pl.ds(0, 8 * (CELLS - 1))
    whole = pltpu.make_async_remote_copy(
        src_ref=sent.at[rest, :],
        dst_ref=got.at[rest, :],
        send_sem=send_sem,
        recv_sem=recv_sem,
        device_id={"cell": lax.rem(me + 1, CELLS)},
        device_id_type=MESH,
    )
    whole.wait_send()
    whole.wait_recv()


def seeds_of(fields, grp, e_seed, s_seed, coef):
    turns, sine, real, imag = fields
    hi = lanes((8, 128)) >= 64
    s1, c1 = sincos_turns(turns)
    e = jnp.where(hi, 0.0, 1.0)
    f = jnp.where(hi, 1.0, 0.0)
    e_seed[pl.ds(8, 8, stride=16), :] = e
    for j in range(1, 9):
        e, f = e * c1 - f * s1, f * c1 + e * s1
        if j < 8:
            e_seed[pl.ds(8 + j, 8, stride=16), :] = e
        e_seed[pl.ds(8 - j, 8, stride=16), :] = jnp.where(hi, -e, e)
    _, c8 = sincos_turns(8.0 * turns)
    coef[0:8, :] = 2.0 * c8
    sa, ca = sincos_turns(0.5 * sine)
    first = (grp * (ANT // 2)).astype(jnp.float32)
    s0, c0 = sincos_turns(first * sine)
    _, a8 = sincos_turns(4.0 * sine)
    coef[8:16, :] = 2.0 * a8
    g1 = jnp.where(hi, -imag, real)
    g2 = jnp.where(hi, real, imag)
    x = g1 * c0 + g2 * s0
    y = g2 * c0 - g1 * s0
    for a in range(16):
        s_seed[pl.ds(a, 8, stride=32), :] = x
        s_seed[pl.ds(16 + a, 8, stride=32), :] = y
        if a < 15:
            x, y = x * ca + y * sa, y * ca - x * sa


def response_of(l, e_seed, s_seed, coef):
    c = jnp.broadcast_to(coef[l : l + 1, :], (8, 128))
    low = e_seed[16 * l : 16 * l + 8, :]
    top = e_seed[16 * l + 8 : 16 * l + 16, :]
    down = [top, low]
    up = [low, top]
    for _ in range(7):
        down.append(c * down[-1] - down[-2])
        up.append(c * up[-1] - up[-2])
    table = jnp.concatenate(down[:0:-1] + up[1:], axis=0).astype(jnp.bfloat16)
    c = jnp.broadcast_to(coef[8 + l : 9 + l, :], (8, 128))
    parts = []
    for h in range(2):
        at = 32 * l + 16 * h
        run = [s_seed[at : at + 8, :], s_seed[at + 8 : at + 16, :]]
        for _ in range(2):
            run.append(c * run[-1] - run[-2])
        parts += run
    spread = jnp.concatenate(parts, axis=0).astype(jnp.bfloat16)
    return lax.dot_general(
        spread, table, (((1,), (1,)), ((), ())), preferred_element_type=jnp.float32
    )


SEED_SCRATCH = [
    pltpu.VMEM((8 * 16, 128), jnp.float32),
    pltpu.VMEM((8 * 32, 128), jnp.float32),
    pltpu.VMEM((16, 128), jnp.float32),
]


def transmit_kernel(
    slots, nearby, got, symbols, rows, weights, tag_v, tag_s, table, raw, serving, e_seed, s_seed, coef, sem
):
    me = lax.axis_index("cell")
    grp = lax.axis_index("grp")
    for c in range(0, CELLS, 8):
        tag_v[c : c + 8, :] = got[pl.ds(8 * c + 4, 8, stride=8), :].astype(jnp.int32)
    copy = pltpu.make_async_copy(tag_v, tag_s, sem)
    copy.start()

    def clear(i, carry):
        raw[pl.ds(pl.multiple_of(64 * i, 64), 64), :] = jnp.zeros((64, 128), jnp.float32)
        return carry

    lax.fori_loop(0, CELL_SECTORS * RESP // 64, clear, 0)
    copy.wait()

    def index(i, carry):
        base = jnp.int32(0)
        for k in range(4):
            tag = tag_s[i, TAG_LANE + 2 * k]
            cnt = tag_s[i, TAG_LANE + 2 * k + 1]
            table[tag] = (i << 16) + (base << 8) + cnt
            base = base + cnt
        return carry

    lax.fori_loop(0, CELLS, index, 0, unroll=4)
    lane = lanes((8, 128))

    def unpack(g, carry):
        code = table[g + 1]
        i = code >> 16
        base = (code >> 8) & 255
        cnt = code & 255
        block = got[pl.ds(pl.multiple_of(8 * i, 8), 8), :]
        turned = pltpu.roll(block, (0 - base) & 127, 1)
        swapped = pltpu.roll(turned, 4, 0)
        value = jnp.where(lane + base >= 128, swapped, turned)
        value = jnp.where(lane < cnt, value, 0.0)
        rows[pl.ds(pl.multiple_of(8 * g, 8), 8), :] = value + pltpu.roll(value, 64, 1)
        return carry

    lax.fori_loop(0, LINKS, unpack, 0, unroll=8)

    def serve(u, carry):
        link = u * NEARBY_COUNT + slots[u]
        serving[pl.ds(pl.multiple_of(8 * u, 8), 8), :] = rows[pl.ds(pl.multiple_of(8 * link, 8), 8), :]
        return carry

    lax.fori_loop(0, USERS, serve, 0, unroll=8)

    def eight_users(c, carry):
        fields = [serving[pl.ds(64 * c + f, 8, stride=8), :] for f in range(4)]
        seeds_of(fields, grp, e_seed, s_seed, coef)
        for l in range(8):
            u = 8 * c + l
            resp = response_of(l, e_seed, s_seed, coef).astype(jnp.bfloat16).astype(jnp.float32)
            sym = symbols[u].astype(jnp.float32)
            sym_r, sym_i = sym[0:1, :], sym[1:2, :]
            real, imag = resp[:ANT, :], resp[ANT:, :]
            part = jnp.concatenate(
                [real * sym_r + imag * sym_i, real * sym_i - imag * sym_r], axis=0
            )
            sector = nearby[slots[u], u] - me * CELL_SECTORS
            at = pl.ds(pl.multiple_of(RESP * sector, RESP), RESP)
            raw[at, :] = raw[at, :] + part
        return carry

    lax.fori_loop(0, USERS // 8, eight_users, 0)

    def normalise(s, carry):
        at = pl.ds(pl.multiple_of(RESP * s, RESP), RESP)
        value = raw[at, :]
        real, imag = value[:ANT, :], value[ANT:, :]
        power = jnp.mean(real * real + imag * imag, axis=1, keepdims=True)
        scale = 1.0 / jnp.sqrt(power + EPSILON)
        weights[s] = jnp.concatenate([real * scale, imag * scale], axis=0).astype(jnp.bfloat16)
        return carry

    lax.fori_loop(0, CELL_SECTORS, normalise, 0, unroll=2)


def receive_kernel(
    nearby, rows, weights, out, near, resp, part, other, e_seed, s_seed, coef, sems
):
    me = lax.axis_index("cell")
    grp = lax.axis_index("grp")
    right = lax.rem(me + 1, CELLS)
    left = lax.rem(me + CELLS - 1, CELLS)
    barrier = pltpu.get_barrier_semaphore()
    for target in ({"cell": left}, {"cell": right}, {"grp": 1 - grp}):
        pl.semaphore_signal(barrier, inc=1, device_id=target, device_id_type=MESH)
    pl.semaphore_wait(barrier, 3)
    to_right = pltpu.make_async_remote_copy(
        src_ref=weights.at[pl.ds(CELL_SECTORS - REACH, REACH)],
        dst_ref=near.at[pl.ds(0, REACH)],
        send_sem=sems.at[0],
        recv_sem=sems.at[1],
        device_id={"cell": right},
        device_id_type=MESH,
    )
    to_left = pltpu.make_async_remote_copy(
        src_ref=weights.at[pl.ds(0, REACH)],
        dst_ref=near.at[pl.ds(REACH + CELL_SECTORS, REACH)],
        send_sem=sems.at[2],
        recv_sem=sems.at[3],
        device_id={"cell": left},
        device_id_type=MESH,
    )
    to_right.start()
    to_left.start()
    keep = pltpu.make_async_copy(weights, near.at[pl.ds(REACH, CELL_SECTORS)], sems.at[4])
    keep.start()

    def respond(u, carry):
        fields = [rows[pl.ds(64 * u + f, 8, stride=8), :] for f in range(4)]
        seeds_of(fields, grp, e_seed, s_seed, coef)
        for l in range(8):
            at = pl.ds(pl.multiple_of(u * (8 * RESP) + RESP * l, RESP), RESP)
            resp[at, :] = response_of(l, e_seed, s_seed, coef).astype(jnp.bfloat16)
        return carry

    lax.fori_loop(0, USERS, respond, 0)
    keep.wait()
    to_right.wait()
    to_left.wait()

    def combine(u, carry):
        real = jnp.zeros((ANT, 128), jnp.float32)
        imag = jnp.zeros((ANT, 128), jnp.float32)
        for k in range(NEARBY_COUNT):
            sector = nearby[k, u] - me * CELL_SECTORS + REACH
            sector = jnp.clip(sector, 0, CELL_SECTORS + 2 * REACH - 1)
            tx = near[sector].astype(jnp.float32)
            at = pl.ds(pl.multiple_of(u * (8 * RESP) + RESP * k, RESP), RESP)
            ch = resp[at, :].astype(jnp.float32)
            real = real + (ch[:ANT] * tx[:ANT] - ch[ANT:] * tx[ANT:])
            imag = imag + (ch[:ANT] * tx[ANT:] + ch[ANT:] * tx[:ANT])
        part[u] = jnp.concatenate(
            [jnp.sum(real, axis=0, keepdims=True), jnp.sum(imag, axis=0, keepdims=True)], axis=0
        )
        return carry

    lax.fori_loop(0, USERS, combine, 0)
    swap = pltpu.make_async_remote_copy(
        src_ref=part,
        dst_ref=other,
        send_sem=sems.at[5],
        recv_sem=sems.at[6],
        device_id={"grp": 1 - grp},
        device_id_type=MESH,
    )
    swap.start()
    swap.wait()
    out[...] = (part[...] + other[...]) * (1.0 / math.sqrt(SECTOR_ANTENNAS))


VMEM = pl.BlockSpec(memory_space=pltpu.VMEM)
SMEM = pl.BlockSpec(memory_space=pltpu.SMEM)


def call(kernel, name, out_shape, in_specs, scratch, remote=None):
    extra = {} if remote is None else {"collective_id": remote, "has_side_effects": True}
    many = isinstance(out_shape, (tuple, list))
    return pl.pallas_call(
        kernel,
        name=name,
        out_shape=out_shape,
        in_specs=in_specs,
        out_specs=[VMEM] * len(out_shape) if many else VMEM,
        scratch_shapes=scratch,
        compiler_params=pltpu.CompilerParams(vmem_limit_bytes=VMEM_LIMIT, **extra),
    )


def shards(
    path_delay,
    path_angle,
    path_gain,
    slot_counts,
    slot_offsets,
    ray_link,
    nearby_sectors,
    serving_slot,
    symbols,
):
    f32, bf16, i32 = jnp.float32, jnp.bfloat16, jnp.int32
    message = jax.ShapeDtypeStruct((CELLS * 8, 128), f32)
    sent = call(
        pack_kernel,
        "pack",
        message,
        [SMEM, SMEM, SMEM, VMEM, VMEM, VMEM],
        [pltpu.VMEM((8 * (PATH_ROWS + 1), 128), f32)],
    )(
        slot_counts,
        slot_offsets,
        ray_link,
        path_delay.reshape(PATH_ROWS, 128),
        path_angle.reshape(PATH_ROWS, 128),
        path_gain,
    )
    got = call(
        exchange_kernel,
        "exchange",
        message,
        [VMEM],
        [pltpu.SemaphoreType.DMA, pltpu.SemaphoreType.DMA],
        remote=0,
    )(sent)
    rows, weights = call(
        transmit_kernel,
        "transmit",
        (
            jax.ShapeDtypeStruct((LINKS * 8, 128), f32),
            jax.ShapeDtypeStruct((CELL_SECTORS, RESP, 128), bf16),
        ),
        [SMEM, SMEM, VMEM, VMEM],
        [
            pltpu.VMEM((CELLS, 128), i32),
            pltpu.SMEM((CELLS, 128), i32),
            pltpu.SMEM((LINKS + 8,), i32),
            pltpu.VMEM((CELL_SECTORS * RESP, 128), f32),
            pltpu.VMEM((USERS * 8, 128), f32),
            *SEED_SCRATCH,
            pltpu.SemaphoreType.DMA,
        ],
    )(serving_slot, nearby_sectors, got, symbols)
    return call(
        receive_kernel,
        "receive",
        jax.ShapeDtypeStruct((USERS, 2, FRAME_TONES), f32),
        [SMEM, VMEM, VMEM],
        [
            pltpu.VMEM((CELL_SECTORS + 2 * REACH, RESP, 128), bf16),
            pltpu.VMEM((LINKS * RESP, 128), bf16),
            pltpu.VMEM((USERS, 2, FRAME_TONES), f32),
            pltpu.VMEM((USERS, 2, FRAME_TONES), f32),
            *SEED_SCRATCH,
            pltpu.SemaphoreType.DMA((7,)),
        ],
        remote=1,
    )(nearby_sectors, rows, weights)


def solution(mesh):
    placed = (
        P("cell"),
        P("cell"),
        P(None, "cell"),
        P("cell"),
        P("cell"),
        P("cell"),
        P(None, "cell"),
        P("cell"),
        P("cell", None, None),
    )
    return jax.shard_map(
        shards, mesh=mesh, in_specs=placed, out_specs=P("cell", None, None), check_vma=False
    )
```

time: 559 us -> 71.9 us (0.13)
  local copies, waits for them, and re-layouts: 425 us -> 3.75 us
  Pallas kernels: 0 us -> 67.8 us
  other arithmetic: 59.4 us -> 0 us
  starting transfers between devices: 33.7 us -> 0 us
  waiting for transfers between devices: 19.4 us -> 0 us
  blocking collectives: 11.8 us -> 0 us
  matrix products: 7.12 us -> 0 us
    gather x18 -> x0, local copies, waits for them, and re-layouts: 383 us -> none  [the longest x8 364 us: shards(): column[where_path]]
    pallas_call x0 -> x4, Pallas kernels: none -> 67.8 us  [the longest x1 26.6 us: shards(): call(exchange_kernel, 'exchange', message, [VMEM], [pltpu.SemaphoreType.D...]
    all_to_all x2 -> x0, starting transfers between devices: 30.2 us -> none  [the longest x1 16.9 us: shards(): lax.all_to_all(link_tags, 'cell', split_axis=1, concat_axis=1, tiled=True)]
    convert_element_type x5 -> x0, other arithmetic: 17.5 us -> none  [the longest x2 16.2 us: make_response(): (imag_rows[:, None, :] * steer_cos - real_rows[:, None, :] * steer_sin).a...]
    neg x2 -> x0, other arithmetic: 15.8 us -> none  [make_response(): upper = jnp.concatenate([spread_real, -spread_imag], axis=2)]
    scatter x1 -> x0, local copies, waits for them, and re-layouts: 14.2 us -> none  [shards(): jnp.zeros((4, link_total, PMAX), jnp.float32).at[:, target, :]]
    all_to_all x2 -> x0, blocking collectives: 11.8 us -> none  [copy_for_each(): return lax.all_to_all(copies, axis, split_axis=0, concat_axis=0, tiled=True)]
    all_to_all x2 -> x0, waiting for transfers between devices: 11.6 us -> none  [the longest x1 11.6 us: shards(): lax.all_to_all(packed, 'cell', split_axis=1, concat_axis=1, tiled=True)]
  transfers between devices with their start and end apart: 4 -> 0, of which waited for: 3 -> 0; matrix products, arithmetic and copies ran while one was open for 67% -> 0% of each run, Pallas kernels for 0% -> 0%
where the time goes in v1:
time: 71.9 us; the launch traced here: 71.7 us
  Pallas kernels  67.8 us (94%)
  local copies, waits for them, and re-layouts  3.75 us (5%)
    pallas_call x1, Pallas kernels, shards(): call(exchange_kernel, 'exchange', message, [VMEM], [pltpu.SemaphoreType.D...  26.6 us
    pallas_call x1, Pallas kernels, shards(): call(receive_kernel, 'receive', jax.ShapeDtypeStruct((USERS, 2, FRAME_TON...  24.7 us
    pallas_call x1, Pallas kernels, shards(): call(transmit_kernel, 'transmit', (jax.ShapeDtypeStruct((LINKS * 8, 128),...  11.9 us
    pallas_call x1, Pallas kernels, shards(): call(pack_kernel, 'pack', message, [SMEM, SMEM, SMEM, VMEM, VMEM, VMEM],...  4.68 us
    unnamed x19, local copies, waits for them, and re-layouts  3.75 us

profile of v1, /device:TPU:1, one launch (start us, length us, event | category | flops | bytes accessed | tf_op | source)
XLA Modules:
  0.0 71.7 jit_solution(11918381011275898753)
XLA Ops:
  0.0 0.0 copy-start.6
  0.0 0.0 copy-start.7
  0.0 0.0 copy-start.5
  0.0 0.7 copy-done.6
  0.7 0.0 copy-done.7
  0.7 0.0 copy-done.5
  0.7 0.0 copy-start
  0.7 0.9 %copy-done = f32[2,8320]{1,0:T(2,128)S(1)} copy-done((f32[2,8320]{1,0:T(2,128)S(1)}, f32[2,8320]{1,0:T(2,128)}, u32[]{:S(2)}) %copy-start) | copy-done | bytes 66584
  1.6 0.0 copy-start.1
  1.6 0.8 %copy-done.1 = f32[8320]{0:T(1024)S(1)} copy-done((f32[8320]{0:T(1024)S(1)}, f32[8320]{0:T(1024)}, u32[]{:S(2)}) %copy-start.1) | copy-done | bytes 33304
  2.4 0.0 copy-start.2
  2.4 0.8 %copy-done.2 = f32[8320]{0:T(1024)S(1)} copy-done((f32[8320]{0:T(1024)S(1)}, f32[8320]{0:T(1024)}, u32[]{:S(2)}) %copy-start.2) | copy-done | bytes 33304
  3.1 4.7 %pack.1.sent = f32[1024,128]{1,0:T(8,128)S(1)} custom-call(s32[256]{0:T(256)S(1)} %copy-done.5, s32[256]{0:T(256)S(1)} %copy-done.6, s32[256]{0:T(256)S(1)} %copy-done.7, f32[65,128]{1,0:T(8,128)S(1)} %bitcast.2, f32[65,128]{1,0:T(8,128)S(1)} %bitcast.3, f32[2,8320]{1,0:T(2,128)S(1)} %copy-done), custom_call_target="tpu_custom_call" | custom-call | tf_op jit(solution)/shard_map/pack/pallas_call | solution.py:393
  7.8 0.0 copy-start.3
  7.8 0.0 copy-start.4
  7.8 0.0 copy-start.8
  7.8 26.6 %exchange.1.got = f32[1024,128]{1,0:T(8,128)S(1)} custom-call(f32[1024,128]{1,0:T(8,128)S(1)} %pack.1.sent), custom_call_target="tpu_custom_call" | custom-call | tf_op jit(solution)/shard_map/exchange/pallas_call | solution.py:407
  34.4 0.0 copy-done.3
  34.4 0.0 copy-done.4
  34.4 0.0 copy-done.8
  34.4 11.9 %transmit.1 = (f32[2048,128]{1,0:T(8,128)S(1)}, bf16[32,64,128]{2,1,0:T(8,128)(2,1)S(1)}) custom-call(s32[32]{0:T(128)S(1)} %copy-done.8, s32[8,32]{1,0:T(8,128)S(1)} %copy-done.3, f32[1024,128]{1,0:T(8,128)S(1)} %exchange.1.got, bf16[32,2,128]{2,1,0:T(2,128)(2,1)S(1)} %copy-done.4), custom_call_target="tpu_custom_call" | custom-call | tf_op jit(solution)/shard_map/transmit/pallas_call | solution.py:415
  46.4 24.7 %receive.1 = f32[32,2,128]{2,1,0:T(2,128)S(1)} custom-call(s32[8,32]{1,0:T(8,128)S(1)} %copy-done.3, f32[2048,128]{1,0:T(8,128)S(1)} %get-tuple-element.7.rows, bf16[32,64,128]{2,1,0:T(8,128)(2,1)S(1)} %get-tuple-element.8.weights), custom_call_target="tpu_custom_call" | custom-call | tf_op jit(solution)/shard_map/receive/pallas_call | solution.py:433
  71.0 0.6 copy.11
Async XLA Ops:
  0.0 0.7 copy-start.6
  0.0 0.7 copy-start.7
  0.0 0.7 copy-start.5
  0.7 0.9 %copy-start = (f32[2,8320]{1,0:T(2,128)S(1)}, f32[2,8320]{1,0:T(2,128)}, u32[]{:S(2)}) copy-start(f32[2,8320]{1,0:T(2,128)} %gain.1) | copy-start | bytes 199684
  1.6 0.8 %copy-start.1 = (f32[8320]{0:T(1024)S(1)}, f32[8320]{0:T(1024)}, u32[]{:S(2)}) copy-start(f32[8320]{0:T(1024)} %param.9) | copy-start | bytes 99844
  2.4 0.8 %copy-start.2 = (f32[8320]{0:T(1024)S(1)}, f32[8320]{0:T(1024)}, u32[]{:S(2)}) copy-start(f32[8320]{0:T(1024)} %param.10) | copy-start | bytes 99844
  7.8 26.6 %copy-start.3 = (s32[8,32]{1,0:T(8,128)S(1)}, s32[8,32]{1,0:T(8,128)}, u32[]{:S(2)}) copy-start(s32[8,32]{1,0:T(8,128)} %nearby.3) | copy-start | bytes 3076
  7.8 26.6 %copy-start.4 = (bf16[32,2,128]{2,1,0:T(2,128)(2,1)S(1)}, bf16[32,2,128]{2,1,0:T(2,128)(2,1)}, u32[]{:S(2)}) copy-start(bf16[32,2,128]{2,1,0:T(2,128)(2,1)} %symbols.1) | copy-start | bytes 49156
  7.8 26.6 %copy-start.8 = (s32[32]{0:T(128)S(1)}, s32[32]{0:T(128)}, u32[]{:S(2)}) copy-start(s32[32]{0:T(128)} %slots.1) | copy-start | bytes 388

commit v2 on v1

--- a/solution.py
+++ b/solution.py
@@ -23,7 +23,9 @@
 ANT = SECTOR_ANTENNAS // 2
 RESP = 2 * ANT
 TAG_LANE = 8
-VMEM_LIMIT = 48 * 1024 * 1024
+HALF = CELLS // 2
+WIRE_ROWS = 5
+MIB = 1024 * 1024
 MESH = pl.DeviceIdType.MESH
 
 
@@ -66,17 +68,31 @@
         out[pl.ds(pl.multiple_of(64 * i, 64), 64), :] = jnp.zeros((64, 128), jnp.float32)
         return carry
 
-    lax.fori_loop(0, CELLS * 8 // 64, clear, 0)
+    lax.fori_loop(0, HALF * 8 // 64, clear, 0)
     lane = lanes((8, 128))
     row = rows_of((8, 128))
     high = row >= 4
     place = lane + jnp.where(high, 128, 0)
     tag_place = jnp.where(row == 4, lane - TAG_LANE, -1000)
+    half = my_half()
+
+    def narrow(_, carry):
+        low, top = carry
+        mid = (low + top) >> 1
+        below = (links[jnp.minimum(mid, SLOTS - 1)] >> 8) < HALF
+        below = below & (low < top)
+        return jnp.where(below, mid + 1, low), jnp.where(below, top, mid)
+
+    split, _ = lax.fori_loop(0, 9, narrow, (jnp.int32(0), jnp.int32(SLOTS)))
+    begin = jnp.where(half == 0, 0, split)
+    end = jnp.where(half == 0, split, SLOTS)
 
     def one(r, carry):
         before, k, base, last = carry
+        live = r < end
+        r = jnp.minimum(r, SLOTS - 1)
         link = links[r]
-        owner = link >> 8
+        owner = jnp.where(live, (link >> 8) - half * HALF, HALF)
         same = owner == before
         k = jnp.where(same, k + 1, 0)
         base = jnp.where(same, base + last, 0)
@@ -97,52 +113,90 @@
         out[at, :] = new
         return owner, k, base, cnt
 
+    def eight(b, carry):
+        for j in range(8):
+            carry = one(begin + 8 * b + j, carry)
+        return carry
+
     zero = jnp.int32(0)
-    lax.fori_loop(0, SLOTS, one, (jnp.int32(-1), zero, zero, zero), unroll=8)
-
-
-def exchange_kernel(sent, got, send_sem, recv_sem):
+    lax.fori_loop(0, (end - begin + 7) >> 3, eight, (jnp.int32(-1), zero, zero, zero))
+    for c in range(0, HALF * 8, 64):
+        extra = [out[pl.ds(c + 4 + f, 8, stride=8), :] for f in range(4)]
+        total = extra[0]
+        for f in range(1, 4):
+            total = total + pltpu.roll(extra[f], 2 * f, 1)
+        out[pl.ds(c + 4, 8, stride=8), :] = total
+
+
+def my_half():
+    return lax.rem(lax.axis_index("grp") + lax.axis_index("cell") // HALF, 2)
+
+
+def exchange_kernel(sent, got, sems):
     me = lax.axis_index("cell")
+    grp = lax.axis_index("grp")
+    start = my_half() * HALF
+    sibling = {"grp": 1 - grp}
     barrier = pltpu.get_barrier_semaphore()
+    pl.semaphore_signal(barrier, inc=1, device_id=sibling, device_id_type=MESH)
 
     def greet(d, carry):
-        other = lax.rem(me + d, CELLS)
+        other = start + lax.rem(me + d, HALF)
         pl.semaphore_signal(barrier, inc=1, device_id={"cell": other}, device_id_type=MESH)
         return carry
 
-    lax.fori_loop(1, CELLS, greet, 0)
-    mine = pl.ds(pl.multiple_of(8 * me, 8), 8)
-    got[mine, :] = sent[mine, :]
-    pl.semaphore_wait(barrier, CELLS - 1)
+    lax.fori_loop(1 - grp, HALF, greet, 0)
+
+    @pl.when(grp == 0)
+    def _():
+        got[me] = sent[lax.rem(me, HALF)]
+
+    pl.semaphore_wait(barrier, HALF + grp)
+    wire = pl.ds(0, WIRE_ROWS)
 
     def send(d, carry):
-        other = lax.rem(me + d, CELLS)
+        near = lax.rem(me + d, HALF)
         pltpu.make_async_remote_copy(
-            src_ref=sent.at[pl.ds(pl.multiple_of(8 * other, 8), 8), :],
-            dst_ref=got.at[mine, :],
-            send_sem=send_sem,
-            recv_sem=recv_sem,
-            device_id={"cell": other},
+            src_ref=sent.at[near, wire],
+            dst_ref=got.at[me, wire],
+            send_sem=sems.at[0],
+            recv_sem=sems.at[1],
+            device_id={"cell": start + near},
             device_id_type=MESH,
         ).start()
         return carry
 
-    lax.fori_loop(1, CELLS, send, 0)
-    rest = pl.ds(0, 8 * (CELLS - 1))
-    whole = pltpu.make_async_remote_copy(
-        src_ref=sent.at[rest, :],
-        dst_ref=got.at[rest, :],
-        send_sem=send_sem,
-        recv_sem=recv_sem,
-        device_id={"cell": lax.rem(me + 1, CELLS)},
+    lax.fori_loop(1 - grp, HALF, send, 0)
+
+    for g in range(2):
+
+        @pl.when(grp == g)
+        def _():
+            whole = pltpu.make_async_remote_copy(
+                src_ref=sent.at[pl.ds(0, HALF - 1 + g), wire],
+                dst_ref=got.at[pl.ds(start, HALF - 1 + g), wire],
+                send_sem=sems.at[0],
+                recv_sem=sems.at[1],
+                device_id=sibling,
+                device_id_type=MESH,
+            )
+            whole.wait_recv()
+            whole.wait_send()
+
+    swap = pltpu.make_async_remote_copy(
+        src_ref=got.at[pl.ds(start, HALF), wire],
+        dst_ref=got.at[pl.ds(start, HALF), wire],
+        send_sem=sems.at[2],
+        recv_sem=sems.at[3],
+        device_id=sibling,
         device_id_type=MESH,
     )
-    whole.wait_send()
-    whole.wait_recv()
+    swap.start()
+    swap.wait()
 
 
 def seeds_of(fields, grp, e_seed, s_seed, coef):
-    turns, sine, real, imag = fields
+    turns, sine, real, imag = [v + pltpu.roll(v, 64, 1) for v in fields]
     hi = lanes((8, 128)) >= 64
     s1, c1 = sincos_turns(turns)
     e = jnp.where(hi, 0.0, 1.0)
@@ -203,12 +257,13 @@
 
 
 def transmit_kernel(
-    slots, nearby, got, symbols, rows, weights, tag_v, tag_s, table, raw, serving, e_seed, s_seed, coef, sem
+    slots, nearby, got, symbols, rows, weights, over, tag_v, tag_s, table, raw, serving, e_seed, s_seed, coef, sem
 ):
     me = lax.axis_index("cell")
     grp = lax.axis_index("grp")
     for c in range(0, CELLS, 8):
-        tag_v[c : c + 8, :] = got[pl.ds(8 * c + 4, 8, stride=8), :].astype(jnp.int32)
+        extra = got[pl.ds(8 * c + 4, 8, stride=8), :]
+        tag_v[c : c + 8, :] = jnp.where(lanes((8, 128)) >= TAG_LANE, extra, 0.0).astype(jnp.int32)
     copy = pltpu.make_async_copy(tag_v, tag_s, sem)
     copy.start()
 
@@ -217,6 +272,10 @@
         return carry
 
     lax.fori_loop(0, CELL_SECTORS * RESP // 64, clear, 0)
+    for c in range(0, CELLS, 8):
+        extra = got[pl.ds(8 * c + 4, 8, stride=8), :]
+        for f in range(4):
+            over[pl.ds(8 * c + f, 8, stride=8), :] = extra if f == 0 else pltpu.roll(extra, 128 - 2 * f, 1)
     copy.wait()
 
     def index(i, carry):
@@ -236,12 +295,10 @@
         i = code >> 16
         base = (code >> 8) & 255
         cnt = code & 255
-        block = got[pl.ds(pl.multiple_of(8 * i, 8), 8), :]
-        turned = pltpu.roll(block, (0 - base) & 127, 1)
-        swapped = pltpu.roll(turned, 4, 0)
-        value = jnp.where(lane + base >= 128, swapped, turned)
-        value = jnp.where(lane < cnt, value, 0.0)
-        rows[pl.ds(pl.multiple_of(8 * g, 8), 8), :] = value + pltpu.roll(value, 64, 1)
+        at = pl.ds(pl.multiple_of(8 * i, 8), 8)
+        value = jnp.where(lane < base + cnt - 128, over[at, :], got[at, :])
+        value = pltpu.roll(value, (0 - base) & 127, 1)
+        rows[pl.ds(pl.multiple_of(8 * g, 8), 8), :] = jnp.where(lane < cnt, value, 0.0)
         return carry
 
     lax.fori_loop(0, LINKS, unpack, 0, unroll=8)
@@ -285,7 +342,8 @@
 
 
 def receive_kernel(
-    nearby, rows, weights, out, near, resp, part, other, e_seed, s_seed, coef, sems
+    nearby, rows, weights, out, near, resp, part, other,
+    e_seed, s_seed, coef, e_seed2, s_seed2, coef2, sems
 ):
     me = lax.axis_index("cell")
     grp = lax.axis_index("grp")
@@ -316,15 +374,26 @@
     keep = pltpu.make_async_copy(weights, near.at[pl.ds(REACH, CELL_SECTORS)], sems.at[4])
     keep.start()
 
-    def respond(u, carry):
-        fields = [rows[pl.ds(64 * u + f, 8, stride=8), :] for f in range(4)]
-        seeds_of(fields, grp, e_seed, s_seed, coef)
+    first, second = (e_seed, s_seed, coef), (e_seed2, s_seed2, coef2)
+
+    def prepare(u, seeds):
+        fields = [rows[pl.ds(pl.multiple_of(64 * u, 64) + f, 8, stride=8), :] for f in range(4)]
+        seeds_of(fields, grp, *seeds)
+
+    def respond(u, seeds):
         for l in range(8):
             at = pl.ds(pl.multiple_of(u * (8 * RESP) + RESP * l, RESP), RESP)
-            resp[at, :] = response_of(l, e_seed, s_seed, coef).astype(jnp.bfloat16)
-        return carry
-
-    lax.fori_loop(0, USERS, respond, 0)
+            resp[at, :] = response_of(l, *seeds).astype(jnp.bfloat16)
+
+    def two_users(v, carry):
+        prepare(2 * v + 1, second)
+        respond(2 * v, first)
+        prepare(jnp.minimum(2 * v + 2, USERS - 1), first)
+        respond(2 * v + 1, second)
+        return carry
+
+    prepare(0, first)
+    lax.fori_loop(0, USERS // 2, two_users, 0)
     keep.wait()
     to_right.wait()
     to_left.wait()
@@ -363,7 +432,7 @@
 SMEM = pl.BlockSpec(memory_space=pltpu.SMEM)
 
 
-def call(kernel, name, out_shape, in_specs, scratch, remote=None):
+def call(kernel, name, mib, out_shape, in_specs, scratch, remote=None):
     extra = {} if remote is None else {"collective_id": remote, "has_side_effects": True}
     many = isinstance(out_shape, (tuple, list))
     return pl.pallas_call(
@@ -373,7 +442,7 @@
         in_specs=in_specs,
         out_specs=[VMEM] * len(out_shape) if many else VMEM,
         scratch_shapes=scratch,
-        compiler_params=pltpu.CompilerParams(vmem_limit_bytes=VMEM_LIMIT, **extra),
+        compiler_params=pltpu.CompilerParams(vmem_limit_bytes=mib * MIB, **extra),
     )
 
 
@@ -389,11 +458,11 @@
     symbols,
 ):
     f32, bf16, i32 = jnp.float32, jnp.bfloat16, jnp.int32
-    message = jax.ShapeDtypeStruct((CELLS * 8, 128), f32)
     sent = call(
         pack_kernel,
         "pack",
-        message,
+        60,
+        jax.ShapeDtypeStruct(((HALF + 1) * 8, 128), f32),
         [SMEM, SMEM, SMEM, VMEM, VMEM, VMEM],
         [pltpu.VMEM((8 * (PATH_ROWS + 1), 128), f32)],
     )(
@@ -407,20 +476,23 @@
     got = call(
         exchange_kernel,
         "exchange",
-        message,
+        16,
+        jax.ShapeDtypeStruct((CELLS, 8, 128), f32),
         [VMEM],
-        [pltpu.SemaphoreType.DMA, pltpu.SemaphoreType.DMA],
+        [pltpu.SemaphoreType.DMA((4,))],
         remote=0,
-    )(sent)
+    )(sent.reshape(HALF + 1, 8, 128))
     rows, weights = call(
         transmit_kernel,
         "transmit",
+        24,
         (
             jax.ShapeDtypeStruct((LINKS * 8, 128), f32),
             jax.ShapeDtypeStruct((CELL_SECTORS, RESP, 128), bf16),
         ),
         [SMEM, SMEM, VMEM, VMEM],
         [
+            pltpu.VMEM((CELLS * 8, 128), f32),
             pltpu.VMEM((CELLS, 128), i32),
             pltpu.SMEM((CELLS, 128), i32),
             pltpu.SMEM((LINKS + 8,), i32),
@@ -429,10 +501,11 @@
             *SEED_SCRATCH,
             pltpu.SemaphoreType.DMA,
         ],
-    )(serving_slot, nearby_sectors, got, symbols)
+    )(serving_slot, nearby_sectors, got.reshape(CELLS * 8, 128), symbols)
     return call(
         receive_kernel,
         "receive",
+        24,
         jax.ShapeDtypeStruct((USERS, 2, FRAME_TONES), f32),
         [SMEM, VMEM, VMEM],
         [
@@ -440,6 +513,7 @@
             pltpu.VMEM((LINKS * RESP, 128), bf16),
             pltpu.VMEM((USERS, 2, FRAME_TONES), f32),
             pltpu.VMEM((USERS, 2, FRAME_TONES), f32),
+            *SEED_SCRATCH,
             *SEED_SCRATCH,
             pltpu.SemaphoreType.DMA((7,)),
         ],

time: 71.9 us -> 55.5 us (0.77)
  Pallas kernels: 67.8 us -> 53.1 us
  local copies, waits for them, and re-layouts: 3.75 us -> 2.21 us
    pallas_call x4, Pallas kernels: 67.8 us -> 53.1 us  [the longest x1 19.5 us: shards(): call(exchange_kernel, 'exchange', 16, jax.ShapeDtypeStruct((CELLS, 8, 128...]
    unnamed x19 -> x9, local copies, waits for them, and re-layouts: 3.75 us -> 2.21 us
where the time goes in v2:
time: 55.5 us; the launch traced here: 55.3 us
  Pallas kernels  53.1 us (96%)
  local copies, waits for them, and re-layouts  2.21 us (4%)
    pallas_call x1, Pallas kernels, shards(): call(exchange_kernel, 'exchange', 16, jax.ShapeDtypeStruct((CELLS, 8, 128...  19.5 us
    pallas_call x1, Pallas kernels, shards(): call(receive_kernel, 'receive', 24, jax.ShapeDtypeStruct((USERS, 2, FRAME...  19.4 us
    pallas_call x1, Pallas kernels, shards(): call(transmit_kernel, 'transmit', 24, (jax.ShapeDtypeStruct((LINKS * 8, 1...  10.1 us
    pallas_call x1, Pallas kernels, shards(): call(pack_kernel, 'pack', 60, jax.ShapeDtypeStruct(((HALF + 1) * 8, 128),...  4.01 us
    unnamed x9, local copies, waits for them, and re-layouts  2.21 us

profile of v2, /device:TPU:1, one launch (start us, length us, event | category | flops | bytes accessed | tf_op | source)
XLA Modules:
  0.0 55.3 jit_solution(13701560526942259128)
XLA Ops:
  0.0 4.0 %pack.1 = f32[520,128]{1,0:T(8,128)} custom-call(s32[256]{0:T(256)} %counts.1, s32[256]{0:T(256)} %offsets.1, s32[256]{0:T(256)} %links.1, f32[65,128]{1,0:T(8,128)} %bitcast.6, f32[65,128]{1,0:T(8,128)} %bitcast.7, f32[2,8320]{1,0:T(2,128)} %gain.1), custom_call_target="tpu_custom_call" | custom-call | tf_op jit(solution)/shard_map/pack/pallas_call | solution.py:461
  4.0 0.0 copy-start
  4.0 0.9 %copy-done = f32[520,128]{1,0:T(8,128)S(1)} copy-done((f32[520,128]{1,0:T(8,128)S(1)}, f32[520,128]{1,0:T(8,128)}, u32[]{:S(2)}) %copy-start) | copy-done | bytes 266264
  5.0 0.0 copy-start.1
  5.0 0.0 copy-start.2
  5.0 19.5 %exchange.1 = f32[128,8,128]{2,1,0:T(8,128)S(1)} custom-call(f32[65,8,128]{2,1,0:T(8,128)S(1)} %bitcast.5), custom_call_target="tpu_custom_call" | custom-call | tf_op jit(solution)/shard_map/exchange/pallas_call | solution.py:476
  24.5 0.0 copy-start.3
  24.5 0.0 copy-done.1
  24.5 0.0 copy-done.2
  24.5 0.6 %copy-done.3 = s32[32]{0:T(128)S(1)} copy-done((s32[32]{0:T(128)S(1)}, s32[32]{0:T(128)}, u32[]{:S(2)}) %copy-start.3) | copy-done | bytes 152
  25.1 10.1 %transmit.1 = (f32[2048,128]{1,0:T(8,128)S(1)}, bf16[32,64,128]{2,1,0:T(8,128)(2,1)S(1)}) custom-call(s32[32]{0:T(128)S(1)} %copy-done.3, s32[8,32]{1,0:T(8,128)S(1)} %copy-done.1, f32[1024,128]{1,0:T(8,128)S(1)} %bitcast.4, bf16[32,2,128]{2,1,0:T(2,128)(2,1)S(1)} %copy-done.2), custom_call_target="tpu_custom_call" | custom-call | tf_op jit(solution)/shard_map/transmit/pallas_call | solution.py:485
  35.3 19.4 %receive.1 = f32[32,2,128]{2,1,0:T(2,128)S(1)} custom-call(s32[8,32]{1,0:T(8,128)S(1)} %copy-done.1, f32[2048,128]{1,0:T(8,128)S(1)} %get-tuple-element.7.rows, bf16[32,64,128]{2,1,0:T(8,128)(2,1)S(1)} %get-tuple-element.8.weights), custom_call_target="tpu_custom_call" | custom-call | tf_op jit(solution)/shard_map/receive/pallas_call | solution.py:505
  54.7 0.6 %copy.11 = f32[32,2,128]{2,1,0:T(2,128)} copy(f32[32,2,128]{2,1,0:T(2,128)S(1)} %receive.1) | data formatting | bytes 65536
Async XLA Ops:
  4.0 1.0 %copy-start = (f32[520,128]{1,0:T(8,128)S(1)}, f32[520,128]{1,0:T(8,128)}, u32[]{:S(2)}) copy-start(f32[520,128]{1,0:T(8,128)} %pack.1) | copy-start | bytes 798724
  5.0 19.5 %copy-start.1 = (s32[8,32]{1,0:T(8,128)S(1)}, s32[8,32]{1,0:T(8,128)}, u32[]{:S(2)}) copy-start(s32[8,32]{1,0:T(8,128)} %nearby.3) | copy-start | bytes 3076
  5.0 19.5 %copy-start.2 = (bf16[32,2,128]{2,1,0:T(2,128)(2,1)S(1)}, bf16[32,2,128]{2,1,0:T(2,128)(2,1)}, u32[]{:S(2)}) copy-start(bf16[32,2,128]{2,1,0:T(2,128)(2,1)} %symbols.1) | copy-start | bytes 49156
  24.5 0.7 %copy-start.3 = (s32[32]{0:T(128)S(1)}, s32[32]{0:T(128)}, u32[]{:S(2)}) copy-start(s32[32]{0:T(128)} %slots.1) | copy-start | bytes 388

commit v3 on v2

--- a/solution.py
+++ b/solution.py
@@ -256,56 +256,54 @@
 ]
 
 
+def unpacked(code, got, over):
+    source = code >> 16
+    base = (code >> 8) & 255
+    cnt = code & 255
+    lane = lanes((8, 128))
+    value = jnp.where(lane < base + cnt - 128, over[source], got[source])
+    return jnp.where(lane < cnt, pltpu.roll(value, (0 - base) & 127, 1), 0.0)
+
+
 def transmit_kernel(
-    slots, nearby, got, symbols, rows, weights, over, tag_v, tag_s, table, raw, serving, e_seed, s_seed, coef, sem
+    slots, nearby, got, symbols, over, table, raw, table_s, serving, e_seed, s_seed, coef, sem
 ):
     me = lax.axis_index("cell")
     grp = lax.axis_index("grp")
-    for c in range(0, CELLS, 8):
-        extra = got[pl.ds(8 * c + 4, 8, stride=8), :]
-        tag_v[c : c + 8, :] = jnp.where(lanes((8, 128)) >= TAG_LANE, extra, 0.0).astype(jnp.int32)
-    copy = pltpu.make_async_copy(tag_v, tag_s, sem)
+    lane = lanes((8, 128))
+    row = rows_of((8, 128))
+    is_tag = (lane >= TAG_LANE) & (lane < TAG_LANE + 8) & (lax.rem(lane, 2) == 0)
+    link = (lane + 1).astype(jnp.float32)
+    found = [jnp.zeros((8, 128), jnp.float32) for _ in range(LINKS // 128)]
+    for c in range(CELLS // 8):
+        extra = got[8 * c : 8 * c + 8, 4, :]
+        for f in range(4):
+            over[8 * c : 8 * c + 8, f, :] = extra if f == 0 else pltpu.roll(extra, 128 - 2 * f, 1)
+        cnt = jnp.where(is_tag, pltpu.roll(extra, 127, 1), 0.0)
+        base = pltpu.roll(cnt, 2, 1) + pltpu.roll(cnt, 4, 1) + pltpu.roll(cnt, 6, 1)
+        code = (8 * c + row).astype(jnp.float32) * 65536.0 + base * 256.0 + cnt
+        for k in range(4):
+            at = TAG_LANE + 2 * k
+            tags = jnp.broadcast_to(extra[:, at : at + 1], (8, 128))
+            codes = jnp.broadcast_to(code[:, at : at + 1], (8, 128))
+            for h in range(LINKS // 128):
+                found[h] = found[h] + jnp.where(tags == link + 128.0 * h, codes, 0.0)
+    for h in range(LINKS // 128):
+        table[h : h + 1, :] = jnp.sum(found[h], axis=0, keepdims=True).astype(jnp.int32)
+    copy = pltpu.make_async_copy(table, table_s, sem)
     copy.start()
 
     def clear(i, carry):
-        raw[pl.ds(pl.multiple_of(64 * i, 64), 64), :] = jnp.zeros((64, 128), jnp.float32)
-        return carry
-
-    lax.fori_loop(0, CELL_SECTORS * RESP // 64, clear, 0)
-    for c in range(0, CELLS, 8):
-        extra = got[pl.ds(8 * c + 4, 8, stride=8), :]
-        for f in range(4):
-            over[pl.ds(8 * c + f, 8, stride=8), :] = extra if f == 0 else pltpu.roll(extra, 128 - 2 * f, 1)
+        raw[i] = jnp.zeros((RESP, 128), jnp.float32)
+        return carry
+
+    lax.fori_loop(0, CELL_SECTORS, clear, 0, unroll=4)
     copy.wait()
 
-    def index(i, carry):
-        base = jnp.int32(0)
-        for k in range(4):
-            tag = tag_s[i, TAG_LANE + 2 * k]
-            cnt = tag_s[i, TAG_LANE + 2 * k + 1]
-            table[tag] = (i << 16) + (base << 8) + cnt
-            base = base + cnt
-        return carry
-
-    lax.fori_loop(0, CELLS, index, 0, unroll=4)
-    lane = lanes((8, 128))
-
-    def unpack(g, carry):
-        code = table[g + 1]
-        i = code >> 16
-        base = (code >> 8) & 255
-        cnt = code & 255
-        at = pl.ds(pl.multiple_of(8 * i, 8), 8)
-        value = jnp.where(lane < base + cnt - 128, over[at, :], got[at, :])
-        value = pltpu.roll(value, (0 - base) & 127, 1)
-        rows[pl.ds(pl.multiple_of(8 * g, 8), 8), :] = jnp.where(lane < cnt, value, 0.0)
-        return carry
-
-    lax.fori_loop(0, LINKS, unpack, 0, unroll=8)
-
     def serve(u, carry):
-        link = u * NEARBY_COUNT + slots[u]
-        serving[pl.ds(pl.multiple_of(8 * u, 8), 8), :] = rows[pl.ds(pl.multiple_of(8 * link, 8), 8), :]
+        g = u * NEARBY_COUNT + slots[u]
+        code = table_s[g >> 7, g & 127]
+        serving[pl.ds(pl.multiple_of(8 * u, 8), 8), :] = unpacked(code, got, over)
         return carry
 
     lax.fori_loop(0, USERS, serve, 0, unroll=8)
@@ -323,27 +321,19 @@
                 [real * sym_r + imag * sym_i, real * sym_i - imag * sym_r], axis=0
             )
             sector = nearby[slots[u], u] - me * CELL_SECTORS
-            at = pl.ds(pl.multiple_of(RESP * sector, RESP), RESP)
-            raw[at, :] = raw[at, :] + part
+            raw[sector] = raw[sector] + part
         return carry
 
     lax.fori_loop(0, USERS // 8, eight_users, 0)
 
-    def normalise(s, carry):
-        at = pl.ds(pl.multiple_of(RESP * s, RESP), RESP)
-        value = raw[at, :]
-        real, imag = value[:ANT, :], value[ANT:, :]
-        power = jnp.mean(real * real + imag * imag, axis=1, keepdims=True)
-        scale = 1.0 / jnp.sqrt(power + EPSILON)
-        weights[s] = jnp.concatenate([real * scale, imag * scale], axis=0).astype(jnp.bfloat16)
-        return carry
-
-    lax.fori_loop(0, CELL_SECTORS, normalise, 0, unroll=2)
+
+PIECE = 8
+PIECES = (0, 16, 8, 24)
 
 
 def receive_kernel(
-    nearby, rows, weights, out, near, resp, part, other,
-    e_seed, s_seed, coef, e_seed2, s_seed2, coef2, sems
+    nearby, table, got, over, raw, out, near, resp, part, other,
+    e_seed, s_seed, coef, e_seed2, s_seed2, coef2, rows, rows2, send_sems, recv_sems
 ):
     me = lax.axis_index("cell")
     grp = lax.axis_index("grp")
@@ -352,33 +342,44 @@
     barrier = pltpu.get_barrier_semaphore()
     for target in ({"cell": left}, {"cell": right}, {"grp": 1 - grp}):
         pl.semaphore_signal(barrier, inc=1, device_id=target, device_id_type=MESH)
-    pl.semaphore_wait(barrier, 3)
-    to_right = pltpu.make_async_remote_copy(
-        src_ref=weights.at[pl.ds(CELL_SECTORS - REACH, REACH)],
-        dst_ref=near.at[pl.ds(0, REACH)],
-        send_sem=sems.at[0],
-        recv_sem=sems.at[1],
-        device_id={"cell": right},
-        device_id_type=MESH,
-    )
-    to_left = pltpu.make_async_remote_copy(
-        src_ref=weights.at[pl.ds(0, REACH)],
-        dst_ref=near.at[pl.ds(REACH + CELL_SECTORS, REACH)],
-        send_sem=sems.at[2],
-        recv_sem=sems.at[3],
-        device_id={"cell": left},
-        device_id_type=MESH,
-    )
-    to_right.start()
-    to_left.start()
-    keep = pltpu.make_async_copy(weights, near.at[pl.ds(REACH, CELL_SECTORS)], sems.at[4])
-    keep.start()
+
+    halo = []
+    for n, begin in enumerate(PIECES):
+
+        def normalise(s, carry):
+            real, imag = raw[s, :ANT, :], raw[s, ANT:, :]
+            power = jnp.mean(real * real + imag * imag, axis=1, keepdims=True)
+            scale = 1.0 / jnp.sqrt(power + EPSILON)
+            near[REACH + s] = jnp.concatenate([real * scale, imag * scale], axis=0).astype(jnp.bfloat16)
+            return carry
+
+        lax.fori_loop(begin, begin + PIECE, normalise, 0, unroll=4)
+        if n == 0:
+            pl.semaphore_wait(barrier, 3)
+        to_left = begin < CELL_SECTORS - REACH
+        land = begin + REACH + CELL_SECTORS if to_left else begin + REACH - CELL_SECTORS
+        halo.append(
+            pltpu.make_async_remote_copy(
+                src_ref=near.at[pl.ds(REACH + begin, PIECE)],
+                dst_ref=near.at[pl.ds(land, PIECE)],
+                send_sem=send_sems.at[n],
+                recv_sem=recv_sems.at[n],
+                device_id={"cell": left if to_left else right},
+                device_id_type=MESH,
+            )
+        )
+        halo[-1].start()
 
     first, second = (e_seed, s_seed, coef), (e_seed2, s_seed2, coef2)
 
-    def prepare(u, seeds):
-        fields = [rows[pl.ds(pl.multiple_of(64 * u, 64) + f, 8, stride=8), :] for f in range(4)]
-        seeds_of(fields, grp, *seeds)
+    def unpack(u, rows):
+        u = jnp.minimum(u, USERS - 1)
+        for l in range(8):
+            code = table[u // 16, lax.rem(u, 16) * 8 + l]
+            rows[8 * l : 8 * l + 8, :] = unpacked(code, got, over)
+
+    def prepare(rows, seeds):
+        seeds_of([rows[pl.ds(f, 8, stride=8), :] for f in range(4)], grp, *seeds)
 
     def respond(u, seeds):
         for l in range(8):
@@ -386,17 +387,21 @@
             resp[at, :] = response_of(l, *seeds).astype(jnp.bfloat16)
 
     def two_users(v, carry):
-        prepare(2 * v + 1, second)
+        prepare(rows2, second)
+        unpack(2 * v + 3, rows2)
         respond(2 * v, first)
-        prepare(jnp.minimum(2 * v + 2, USERS - 1), first)
+        prepare(rows, first)
+        unpack(2 * v + 4, rows)
         respond(2 * v + 1, second)
         return carry
 
-    prepare(0, first)
+    unpack(0, rows)
+    prepare(rows, first)
+    unpack(1, rows2)
+    unpack(2, rows)
     lax.fori_loop(0, USERS // 2, two_users, 0)
-    keep.wait()
-    to_right.wait()
-    to_left.wait()
+    for copy in halo:
+        copy.wait()
 
     def combine(u, carry):
         real = jnp.zeros((ANT, 128), jnp.float32)
@@ -418,8 +423,8 @@
     swap = pltpu.make_async_remote_copy(
         src_ref=part,
         dst_ref=other,
-        send_sem=sems.at[5],
-        recv_sem=sems.at[6],
+        send_sem=send_sems.at[len(PIECES)],
+        recv_sem=recv_sems.at[len(PIECES)],
         device_id={"grp": 1 - grp},
         device_id_type=MESH,
     )
@@ -482,32 +487,29 @@
         [pltpu.SemaphoreType.DMA((4,))],
         remote=0,
     )(sent.reshape(HALF + 1, 8, 128))
-    rows, weights = call(
+    over, table, raw = call(
         transmit_kernel,
         "transmit",
         24,
         (
-            jax.ShapeDtypeStruct((LINKS * 8, 128), f32),
-            jax.ShapeDtypeStruct((CELL_SECTORS, RESP, 128), bf16),
+            jax.ShapeDtypeStruct((CELLS, 8, 128), f32),
+            jax.ShapeDtypeStruct((LINKS // 128, 128), i32),
+            jax.ShapeDtypeStruct((CELL_SECTORS, RESP, 128), f32),
         ),
         [SMEM, SMEM, VMEM, VMEM],
         [
-            pltpu.VMEM((CELLS * 8, 128), f32),
-            pltpu.VMEM((CELLS, 128), i32),
-            pltpu.SMEM((CELLS, 128), i32),
-            pltpu.SMEM((LINKS + 8,), i32),
-            pltpu.VMEM((CELL_SECTORS * RESP, 128), f32),
+            pltpu.SMEM((LINKS // 128, 128), i32),
             pltpu.VMEM((USERS * 8, 128), f32),
             *SEED_SCRATCH,
             pltpu.SemaphoreType.DMA,
         ],
-    )(serving_slot, nearby_sectors, got.reshape(CELLS * 8, 128), symbols)
+    )(serving_slot, nearby_sectors, got, symbols)
     return call(
         receive_kernel,
         "receive",
         24,
         jax.ShapeDtypeStruct((USERS, 2, FRAME_TONES), f32),
-        [SMEM, VMEM, VMEM],
+        [SMEM, SMEM, VMEM, VMEM, VMEM],
         [
             pltpu.VMEM((CELL_SECTORS + 2 * REACH, RESP, 128), bf16),
             pltpu.VMEM((LINKS * RESP, 128), bf16),
@@ -515,10 +517,13 @@
             pltpu.VMEM((USERS, 2, FRAME_TONES), f32),
             *SEED_SCRATCH,
             *SEED_SCRATCH,
-            pltpu.SemaphoreType.DMA((7,)),
+            pltpu.VMEM((64, 128), f32),
+            pltpu.VMEM((64, 128), f32),
+            pltpu.SemaphoreType.DMA((len(PIECES) + 1,)),
+            pltpu.SemaphoreType.DMA((len(PIECES) + 1,)),
         ],
         remote=1,
-    )(nearby_sectors, rows, weights)
+    )(nearby_sectors, table, got, over, raw)
 
 
 def solution(mesh):

time: 55.5 us -> 52.4 us (0.944)
  Pallas kernels: 53.1 us -> 50.7 us
  local copies, waits for them, and re-layouts: 2.21 us -> 1.58 us
    pallas_call x1, Pallas kernels: 10.1 us -> 6.04 us  [shards(): call(transmit_kernel, 'transmit', 24, (jax.ShapeDtypeStruct((CELLS, 8, 12...]
    pallas_call x1, Pallas kernels: 19.4 us -> 20.9 us  [shards(): call(receive_kernel, 'receive', 24, jax.ShapeDtypeStruct((USERS, 2, FRAME...]
    unnamed x9, local copies, waits for them, and re-layouts: 2.21 us -> 1.58 us
where the time goes in v3:
time: 52.4 us; the launch traced here: 52.3 us
  Pallas kernels  50.7 us (97%)
  local copies, waits for them, and re-layouts  1.58 us (3%)
    pallas_call x1, Pallas kernels, shards(): call(receive_kernel, 'receive', 24, jax.ShapeDtypeStruct((USERS, 2, FRAME...  20.9 us
    pallas_call x1, Pallas kernels, shards(): call(exchange_kernel, 'exchange', 16, jax.ShapeDtypeStruct((CELLS, 8, 128...  19.6 us
    pallas_call x1, Pallas kernels, shards(): call(transmit_kernel, 'transmit', 24, (jax.ShapeDtypeStruct((CELLS, 8, 12...  6.04 us
    pallas_call x1, Pallas kernels, shards(): call(pack_kernel, 'pack', 60, jax.ShapeDtypeStruct(((HALF + 1) * 8, 128),...  4.14 us
    unnamed x9, local copies, waits for them, and re-layouts  1.58 us

profile of v3, /device:TPU:1, one launch (start us, length us, event | category | flops | bytes accessed | tf_op | source)
XLA Modules:
  0.0 52.3 jit_solution(5739364232264057081)
XLA Ops:
  0.0 4.1 %pack.1 = f32[520,128]{1,0:T(8,128)} custom-call(s32[256]{0:T(256)} %counts.1, s32[256]{0:T(256)} %offsets.1, s32[256]{0:T(256)} %links.1, f32[65,128]{1,0:T(8,128)} %bitcast.4, f32[65,128]{1,0:T(8,128)} %bitcast.5, f32[2,8320]{1,0:T(2,128)} %gain.1), custom_call_target="tpu_custom_call" | custom-call | tf_op jit(solution)/shard_map/pack/pallas_call | solution.py:466
  4.1 0.0 copy-start
  4.1 0.9 %copy-done = f32[520,128]{1,0:T(8,128)S(1)} copy-done((f32[520,128]{1,0:T(8,128)S(1)}, f32[520,128]{1,0:T(8,128)}, u32[]{:S(2)}) %copy-start) | copy-done | bytes 266264
  5.1 0.0 copy-start.1
  5.1 0.0 copy-start.2
  5.1 0.0 copy-start.3
  5.1 19.6 %exchange.1.got = f32[128,8,128]{2,1,0:T(8,128)S(1)} custom-call(f32[65,8,128]{2,1,0:T(8,128)S(1)} %bitcast.3), custom_call_target="tpu_custom_call" | custom-call | tf_op jit(solution)/shard_map/exchange/pallas_call | solution.py:481
  24.7 0.0 copy-done.1
  24.7 0.0 copy-done.2
  24.7 0.0 copy-done.3
  24.7 6.0 %transmit.1 = (f32[128,8,128]{2,1,0:T(8,128)S(1)}, s32[2,128]{1,0:T(2,128)S(1)}, f32[32,64,128]{2,1,0:T(8,128)S(1)}) custom-call(s32[32]{0:T(128)S(1)} %copy-done.3, s32[8,32]{1,0:T(8,128)S(1)} %copy-done.1, f32[128,8,128]{2,1,0:T(8,128)S(1)} %exchange.1.got, bf16[32,2,128]{2,1,0:T(2,128)(2,1)S(1)} %copy-done.2), custom_call_target="tpu_custom_call" | custom-call | tf_op jit(solution)/shard_map/transmit/pallas_call | solution.py:490
  30.8 20.9 %receive.1 = f32[32,2,128]{2,1,0:T(2,128)S(1)} custom-call(s32[8,32]{1,0:T(8,128)S(1)} %copy-done.1, s32[2,128]{1,0:T(2,128)S(1)} %get-tuple-element.8.table, f32[128,8,128]{2,1,0:T(8,128)S(1)} %exchange.1.got, f32[128,8,128]{2,1,0:T(8,128)S(1)} %get-tuple-element.9.over, f32[32,64,128]{2,1,0:T(8,128)S(1)} %get-tuple-element.10.raw), custom_call_target="tpu_custom_call" | custom-call | tf_op jit(solution)/shard_map/receive/pallas_call | solution.py:507
  51.7 0.6 %copy.11 = f32[32,2,128]{2,1,0:T(2,128)} copy(f32[32,2,128]{2,1,0:T(2,128)S(1)} %receive.1) | data formatting | bytes 65536
Async XLA Ops:
  4.1 1.0 %copy-start = (f32[520,128]{1,0:T(8,128)S(1)}, f32[520,128]{1,0:T(8,128)}, u32[]{:S(2)}) copy-start(f32[520,128]{1,0:T(8,128)} %pack.1) | copy-start | bytes 798724
  5.1 19.6 %copy-start.1 = (s32[8,32]{1,0:T(8,128)S(1)}, s32[8,32]{1,0:T(8,128)}, u32[]{:S(2)}) copy-start(s32[8,32]{1,0:T(8,128)} %nearby.3) | copy-start | bytes 3076
  5.1 19.6 %copy-start.2 = (bf16[32,2,128]{2,1,0:T(2,128)(2,1)S(1)}, bf16[32,2,128]{2,1,0:T(2,128)(2,1)}, u32[]{:S(2)}) copy-start(bf16[32,2,128]{2,1,0:T(2,128)(2,1)} %symbols.1) | copy-start | bytes 49156
  5.1 19.6 %copy-start.3 = (s32[32]{0:T(128)S(1)}, s32[32]{0:T(128)}, u32[]{:S(2)}) copy-start(s32[32]{0:T(128)} %slots.1) | copy-start | bytes 388

commit v4 on v3

--- a/solution.py
+++ b/solution.py
@@ -51,101 +51,102 @@
     return 2.0 * sh * ch, 1.0 - 2.0 * sh * sh
 
 
-def pack_kernel(counts, offsets, links, delay, angle, gain, out, store):
+def my_half():
+    return lax.rem(lax.axis_index("grp") + lax.axis_index("cell") // HALF, 2)
+
+
+def deliver_kernel(
+    counts, offsets, links, delay_in, angle_in, gain_in, got,
+    delay, angle, gain, store, sent, begins, load_sems, sems
+):
+    me = lax.axis_index("cell")
+    grp = lax.axis_index("grp")
+    start = my_half() * HALF
+    sibling = {"grp": 1 - grp}
+    loads = [
+        pltpu.make_async_copy(src, dst, load_sems.at[n])
+        for n, (src, dst) in enumerate(((delay_in, delay), (angle_in, angle), (gain_in, gain)))
+    ]
+    for copy in loads:
+        copy.start()
+    barrier = pltpu.get_barrier_semaphore()
+    pl.semaphore_signal(barrier, inc=1, device_id=sibling, device_id_type=MESH)
+
+    def greet(d, carry):
+        other = start + lax.rem(me + d, HALF)
+        pl.semaphore_signal(barrier, inc=1, device_id={"cell": other}, device_id_type=MESH)
+        return carry
+
+    lax.fori_loop(1 - grp, HALF, greet, 0)
+
+    def narrow(_, carry):
+        low, top = carry
+        mid = (low + top) >> 1
+        below = (links[jnp.minimum(mid, SLOTS - 1)] >> 8) < start
+        below = below & (low < top)
+        return jnp.where(below, mid + 1, low), jnp.where(below, top, mid)
+
+    at, _ = lax.fori_loop(0, 9, narrow, (jnp.int32(0), jnp.int32(SLOTS)))
+
+    def count(o, at):
+        begins[o] = at
+        total = at
+        for k in range(4):
+            slot = at + k
+            mine = (links[jnp.minimum(slot, SLOTS - 1)] >> 8) == start + o
+            total = total + jnp.where(mine & (slot < SLOTS), 1, 0)
+        return total
+
+    begins[HALF] = lax.fori_loop(0, HALF, count, at, unroll=4)
+
+    for copy in loads:
+        copy.wait()
     for c in range(0, PATH_ROWS, 8):
         n = min(8, PATH_ROWS - c)
         for f, ref in ((0, delay), (1, angle)):
             value = ref[c : c + n, :]
             value = value * (1.0 / FRAME_TONES) if f == 0 else jnp.sin(value)
-            store[pl.ds(8 * (c + 1) + f, n, stride=8), :] = value
-            store[pl.ds(8 * c + 4 + f, n, stride=8), :] = value
+            store[c : c + n, f, :] = value
+            store[c : c + n, 4 + f, :] = value
     for q in range(PATH_ROWS):
         pair = gain[:, 128 * q : 128 * (q + 1)]
-        store[8 * (q + 1) + 2 : 8 * (q + 1) + 4, :] = pair
-        store[8 * q + 6 : 8 * q + 8, :] = pair
-
-    def clear(i, carry):
-        out[pl.ds(pl.multiple_of(64 * i, 64), 64), :] = jnp.zeros((64, 128), jnp.float32)
-        return carry
-
-    lax.fori_loop(0, HALF * 8 // 64, clear, 0)
+        store[q, 2:4, :] = pair
+        store[q, 6:8, :] = pair
+    store[PATH_ROWS] = jnp.zeros((8, 128), jnp.float32)
+
     lane = lanes((8, 128))
     row = rows_of((8, 128))
-    high = row >= 4
-    place = lane + jnp.where(high, 128, 0)
+    place = lane + jnp.where(row >= 4, 128, 0)
     tag_place = jnp.where(row == 4, lane - TAG_LANE, -1000)
-    half = my_half()
-
-    def narrow(_, carry):
-        low, top = carry
-        mid = (low + top) >> 1
-        below = (links[jnp.minimum(mid, SLOTS - 1)] >> 8) < HALF
-        below = below & (low < top)
-        return jnp.where(below, mid + 1, low), jnp.where(below, top, mid)
-
-    split, _ = lax.fori_loop(0, 9, narrow, (jnp.int32(0), jnp.int32(SLOTS)))
-    begin = jnp.where(half == 0, 0, split)
-    end = jnp.where(half == 0, split, SLOTS)
-
-    def one(r, carry):
-        before, k, base, last = carry
-        live = r < end
-        r = jnp.minimum(r, SLOTS - 1)
-        link = links[r]
-        owner = jnp.where(live, (link >> 8) - half * HALF, HALF)
-        same = owner == before
-        k = jnp.where(same, k + 1, 0)
-        base = jnp.where(same, base + last, 0)
-        off = offsets[r]
-        cnt = counts[r]
-        q = off >> 7
-        s = off & 127
-        block = store[pl.ds(pl.multiple_of(8 * q + 8, 8), 8), :]
-        turned = pltpu.roll(block, (base - s) & 127, 1)
-        swapped = pltpu.roll(turned, 4, 0)
-        j = place - base
-        second = (j + s) >= 128
-        value = jnp.where(second == high, turned, swapped)
-        at = pl.ds(pl.multiple_of(8 * owner, 8), 8)
-        new = jnp.where((j >= 0) & (j < cnt), value, out[at, :])
-        new = jnp.where(tag_place == 2 * k, ((link & 255) + 1).astype(jnp.float32), new)
-        new = jnp.where(tag_place == 2 * k + 1, cnt.astype(jnp.float32), new)
-        out[at, :] = new
-        return owner, k, base, cnt
-
-    def eight(b, carry):
-        for j in range(8):
-            carry = one(begin + 8 * b + j, carry)
-        return carry
-
-    zero = jnp.int32(0)
-    lax.fori_loop(0, (end - begin + 7) >> 3, eight, (jnp.int32(-1), zero, zero, zero))
-    for c in range(0, HALF * 8, 64):
-        extra = [out[pl.ds(c + 4 + f, 8, stride=8), :] for f in range(4)]
-        total = extra[0]
+
+    def pack(o, carry):
+        first = begins[o]
+        number = begins[o + 1] - first
+        base = jnp.int32(0)
+        message = jnp.zeros((8, 128), jnp.float32)
+        for k in range(4):
+            r = jnp.minimum(first + k, SLOTS - 1)
+            cnt = jnp.where(k < number, counts[r], 0)
+            tag = jnp.where(k < number, (links[r] & 255) + 1, 0)
+            off = offsets[r]
+            q = off >> 7
+            s = off & 127
+            value = jnp.where(lane < s + cnt - 128, store[q + 1], store[q])
+            value = pltpu.roll(value, (base - s) & 127, 1)
+            j = place - base
+            message = jnp.where((j >= 0) & (j < cnt), value, message)
+            message = jnp.where(tag_place == 2 * k, tag.astype(jnp.float32), message)
+            message = jnp.where(tag_place == 2 * k + 1, cnt.astype(jnp.float32), message)
+            base = base + cnt
+        sent[o] = message
+        return carry
+
+    lax.fori_loop(0, HALF, pack, 0, unroll=4)
+    for c in range(0, HALF, 8):
+        total = sent[c : c + 8, 4, :]
         for f in range(1, 4):
-            total = total + pltpu.roll(extra[f], 2 * f, 1)
-        out[pl.ds(c + 4, 8, stride=8), :] = total
-
-
-def my_half():
-    return lax.rem(lax.axis_index("grp") + lax.axis_index("cell") // HALF, 2)
-
-
-def exchange_kernel(sent, got, sems):
-    me = lax.axis_index("cell")
-    grp = lax.axis_index("grp")
-    start = my_half() * HALF
-    sibling = {"grp": 1 - grp}
-    barrier = pltpu.get_barrier_semaphore()
-    pl.semaphore_signal(barrier, inc=1, device_id=sibling, device_id_type=MESH)
-
-    def greet(d, carry):
-        other = start + lax.rem(me + d, HALF)
-        pl.semaphore_signal(barrier, inc=1, device_id={"cell": other}, device_id_type=MESH)
-        return carry
-
-    lax.fori_loop(1 - grp, HALF, greet, 0)
+            total = total + pltpu.roll(sent[c : c + 8, 4 + f, :], 2 * f, 1)
+        sent[c : c + 8, 4, :] = total
 
     @pl.when(grp == 0)
     def _():
@@ -435,6 +436,7 @@
 
 VMEM = pl.BlockSpec(memory_space=pltpu.VMEM)
 SMEM = pl.BlockSpec(memory_space=pltpu.SMEM)
+HBM = pl.BlockSpec(memory_space=pltpu.HBM)
 
 
 def call(kernel, name, mib, out_shape, in_specs, scratch, remote=None):
@@ -463,13 +465,23 @@
     symbols,
 ):
     f32, bf16, i32 = jnp.float32, jnp.bfloat16, jnp.int32
-    sent = call(
-        pack_kernel,
-        "pack",
+    got = call(
+        deliver_kernel,
+        "deliver",
         60,
-        jax.ShapeDtypeStruct(((HALF + 1) * 8, 128), f32),
-        [SMEM, SMEM, SMEM, VMEM, VMEM, VMEM],
-        [pltpu.VMEM((8 * (PATH_ROWS + 1), 128), f32)],
+        jax.ShapeDtypeStruct((CELLS, 8, 128), f32),
+        [SMEM, SMEM, SMEM, HBM, HBM, HBM],
+        [
+            pltpu.VMEM((PATH_ROWS, 128), f32),
+            pltpu.VMEM((PATH_ROWS, 128), f32),
+            pltpu.VMEM((2, PATH_ROWS * 128), f32),
+            pltpu.VMEM((PATH_ROWS + 1, 8, 128), f32),
+            pltpu.VMEM((HALF, 8, 128), f32),
+            pltpu.SMEM((HALF + 1,), i32),
+            pltpu.SemaphoreType.DMA((3,)),
+            pltpu.SemaphoreType.DMA((4,)),
+        ],
+        remote=0,
     )(
         slot_counts,
         slot_offsets,
@@ -478,15 +490,6 @@
         path_angle.reshape(PATH_ROWS, 128),
         path_gain,
     )
-    got = call(
-        exchange_kernel,
-        "exchange",
-        16,
-        jax.ShapeDtypeStruct((CELLS, 8, 128), f32),
-        [VMEM],
-        [pltpu.SemaphoreType.DMA((4,))],
-        remote=0,
-    )(sent.reshape(HALF + 1, 8, 128))
     over, table, raw = call(
         transmit_kernel,
         "transmit",

time: 52.4 us -> 50.3 us (0.960)
  Pallas kernels: 50.7 us -> 48.4 us
    pallas_call x1, Pallas kernels: 20.9 us -> 19.3 us  [shards(): call(receive_kernel, 'receive', 24, jax.ShapeDtypeStruct((USERS, 2, FRAME...]
    pallas_call x2 -> x1, Pallas kernels: 23.7 us -> 23 us  [shards(): call(deliver_kernel, 'deliver', 60, jax.ShapeDtypeStruct((CELLS, 8, 128),...]
where the time goes in v4:
time: 50.3 us; the launch traced here: 50.1 us
  Pallas kernels  48.4 us (96%)
  local copies, waits for them, and re-layouts  1.66 us (3%)
    pallas_call x1, Pallas kernels, shards(): call(deliver_kernel, 'deliver', 60, jax.ShapeDtypeStruct((CELLS, 8, 128),...  23 us
    pallas_call x1, Pallas kernels, shards(): call(receive_kernel, 'receive', 24, jax.ShapeDtypeStruct((USERS, 2, FRAME...  19.3 us
    pallas_call x1, Pallas kernels, shards(): call(transmit_kernel, 'transmit', 24, (jax.ShapeDtypeStruct((CELLS, 8, 12...  6.04 us
    unnamed x9, local copies, waits for them, and re-layouts  1.66 us

profile of v4, /device:TPU:1, one launch (start us, length us, event | category | flops | bytes accessed | tf_op | source)
XLA Modules:
  0.0 50.1 jit_solution(8641802391802531786)
XLA Ops:
  0.0 0.0 copy-start.1
  0.0 0.0 copy-start.2
  0.0 0.0 copy-start.3
  0.0 23.0 %deliver.1.got = f32[128,8,128]{2,1,0:T(8,128)} custom-call(s32[256]{0:T(256)} %counts.1, s32[256]{0:T(256)} %offsets.1, s32[256]{0:T(256)} %links.1, f32[65,128]{1,0:T(8,128)} %bitcast.2, f32[65,128]{1,0:T(8,128)} %bitcast.3, f32[2,8320]{1,0:T(2,128)} %gain_in.1), custom_call_target="tpu_custom_call" | custom-call | tf_op jit(solution)/shard_map/deliver/pallas_call | solution.py:468
  23.1 0.0 copy-done.1
  23.1 0.0 copy-done.2
  23.1 0.0 copy-done.3
  23.1 0.0 copy-start
  23.1 1.0 %copy-done = f32[128,8,128]{2,1,0:T(8,128)S(1)} copy-done((f32[128,8,128]{2,1,0:T(8,128)S(1)}, f32[128,8,128]{2,1,0:T(8,128)}, u32[]{:S(2)}) %copy-start) | copy-done | bytes 524312
  24.1 6.0 %transmit.1 = (f32[128,8,128]{2,1,0:T(8,128)S(1)}, s32[2,128]{1,0:T(2,128)S(1)}, f32[32,64,128]{2,1,0:T(8,128)S(1)}) custom-call(s32[32]{0:T(128)S(1)} %copy-done.3, s32[8,32]{1,0:T(8,128)S(1)} %copy-done.1, f32[128,8,128]{2,1,0:T(8,128)S(1)} %copy-done, bf16[32,2,128]{2,1,0:T(2,128)(2,1)S(1)} %copy-done.2), custom_call_target="tpu_custom_call" | custom-call | tf_op jit(solution)/shard_map/transmit/pallas_call | solution.py:493
  30.2 19.3 %receive.1 = f32[32,2,128]{2,1,0:T(2,128)S(1)} custom-call(s32[8,32]{1,0:T(8,128)S(1)} %copy-done.1, s32[2,128]{1,0:T(2,128)S(1)} %get-tuple-element.8.table, f32[128,8,128]{2,1,0:T(8,128)S(1)} %copy-done, f32[128,8,128]{2,1,0:T(8,128)S(1)} %get-tuple-element.9.over, f32[32,64,128]{2,1,0:T(8,128)S(1)} %get-tuple-element.10.raw), custom_call_target="tpu_custom_call" | custom-call | tf_op jit(solution)/shard_map/receive/pallas_call | solution.py:510
  49.5 0.6 %copy.11 = f32[32,2,128]{2,1,0:T(2,128)} copy(f32[32,2,128]{2,1,0:T(2,128)S(1)} %receive.1) | data formatting | bytes 65536
Async XLA Ops:
  0.0 23.1 %copy-start.1 = (s32[8,32]{1,0:T(8,128)S(1)}, s32[8,32]{1,0:T(8,128)}, u32[]{:S(2)}) copy-start(s32[8,32]{1,0:T(8,128)} %nearby.3) | copy-start | bytes 3076
  0.0 23.1 %copy-start.2 = (bf16[32,2,128]{2,1,0:T(2,128)(2,1)S(1)}, bf16[32,2,128]{2,1,0:T(2,128)(2,1)}, u32[]{:S(2)}) copy-start(bf16[32,2,128]{2,1,0:T(2,128)(2,1)} %symbols.1) | copy-start | bytes 49156
  0.0 23.1 %copy-start.3 = (s32[32]{0:T(128)S(1)}, s32[32]{0:T(128)}, u32[]{:S(2)}) copy-start(s32[32]{0:T(128)} %slots.1) | copy-start | bytes 388
  23.1 1.0 %copy-start = (f32[128,8,128]{2,1,0:T(8,128)S(1)}, f32[128,8,128]{2,1,0:T(8,128)}, u32[]{:S(2)}) copy-start(f32[128,8,128]{2,1,0:T(8,128)} %deliver.1.got) | copy-start | bytes 1572868

commit v5 on v4

--- a/solution.py
+++ b/solution.py
@@ -56,19 +56,12 @@
 
 
 def deliver_kernel(
-    counts, offsets, links, delay_in, angle_in, gain_in, got,
-    delay, angle, gain, store, sent, begins, load_sems, sems
+    counts, offsets, links, fields, got, store, sent, begins, sems
 ):
     me = lax.axis_index("cell")
     grp = lax.axis_index("grp")
     start = my_half() * HALF
     sibling = {"grp": 1 - grp}
-    loads = [
-        pltpu.make_async_copy(src, dst, load_sems.at[n])
-        for n, (src, dst) in enumerate(((delay_in, delay), (angle_in, angle), (gain_in, gain)))
-    ]
-    for copy in loads:
-        copy.start()
     barrier = pltpu.get_barrier_semaphore()
     pl.semaphore_signal(barrier, inc=1, device_id=sibling, device_id_type=MESH)
 
@@ -99,19 +92,14 @@
 
     begins[HALF] = lax.fori_loop(0, HALF, count, at, unroll=4)
 
-    for copy in loads:
-        copy.wait()
     for c in range(0, PATH_ROWS, 8):
         n = min(8, PATH_ROWS - c)
-        for f, ref in ((0, delay), (1, angle)):
-            value = ref[c : c + n, :]
-            value = value * (1.0 / FRAME_TONES) if f == 0 else jnp.sin(value)
+        for f in range(4):
+            value = fields[f, c : c + n, :]
+            if f < 2:
+                value = value * (1.0 / FRAME_TONES) if f == 0 else jnp.sin(value)
             store[c : c + n, f, :] = value
             store[c : c + n, 4 + f, :] = value
-    for q in range(PATH_ROWS):
-        pair = gain[:, 128 * q : 128 * (q + 1)]
-        store[q, 2:4, :] = pair
-        store[q, 6:8, :] = pair
     store[PATH_ROWS] = jnp.zeros((8, 128), jnp.float32)
 
     lane = lanes((8, 128))
@@ -267,7 +255,8 @@
 
 
 def transmit_kernel(
-    slots, nearby, got, symbols, over, table, raw, table_s, serving, e_seed, s_seed, coef, sem
+    slots, nearby, got, symbols, over, table, raw, table_s, serving,
+    e_seed, s_seed, coef, e_seed2, s_seed2, coef2, sem
 ):
     me = lax.axis_index("cell")
     grp = lax.axis_index("grp")
@@ -309,12 +298,19 @@
 
     lax.fori_loop(0, USERS, serve, 0, unroll=8)
 
-    def eight_users(c, carry):
+    seeds = (e_seed, s_seed, coef), (e_seed2, s_seed2, coef2)
+
+    def prepare(c):
         fields = [serving[pl.ds(64 * c + f, 8, stride=8), :] for f in range(4)]
-        seeds_of(fields, grp, e_seed, s_seed, coef)
+        seeds_of(fields, grp, *seeds[c % 2])
+
+    prepare(0)
+    for c in range(USERS // 8):
+        if c + 1 < USERS // 8:
+            prepare(c + 1)
         for l in range(8):
             u = 8 * c + l
-            resp = response_of(l, e_seed, s_seed, coef).astype(jnp.bfloat16).astype(jnp.float32)
+            resp = response_of(l, *seeds[c % 2]).astype(jnp.bfloat16).astype(jnp.float32)
             sym = symbols[u].astype(jnp.float32)
             sym_r, sym_i = sym[0:1, :], sym[1:2, :]
             real, imag = resp[:ANT, :], resp[ANT:, :]
@@ -323,9 +319,6 @@
             )
             sector = nearby[slots[u], u] - me * CELL_SECTORS
             raw[sector] = raw[sector] + part
-        return carry
-
-    lax.fori_loop(0, USERS // 8, eight_users, 0)
 
 
 PIECE = 8
@@ -436,7 +429,6 @@
 
 VMEM = pl.BlockSpec(memory_space=pltpu.VMEM)
 SMEM = pl.BlockSpec(memory_space=pltpu.SMEM)
-HBM = pl.BlockSpec(memory_space=pltpu.HBM)
 
 
 def call(kernel, name, mib, out_shape, in_specs, scratch, remote=None):
@@ -468,17 +460,13 @@
     got = call(
         deliver_kernel,
         "deliver",
-        60,
+        16,
         jax.ShapeDtypeStruct((CELLS, 8, 128), f32),
-        [SMEM, SMEM, SMEM, HBM, HBM, HBM],
+        [SMEM, SMEM, SMEM, VMEM],
         [
-            pltpu.VMEM((PATH_ROWS, 128), f32),
-            pltpu.VMEM((PATH_ROWS, 128), f32),
-            pltpu.VMEM((2, PATH_ROWS * 128), f32),
             pltpu.VMEM((PATH_ROWS + 1, 8, 128), f32),
             pltpu.VMEM((HALF, 8, 128), f32),
             pltpu.SMEM((HALF + 1,), i32),
-            pltpu.SemaphoreType.DMA((3,)),
             pltpu.SemaphoreType.DMA((4,)),
         ],
         remote=0,
@@ -486,9 +474,7 @@
         slot_counts,
         slot_offsets,
         ray_link,
-        path_delay.reshape(PATH_ROWS, 128),
-        path_angle.reshape(PATH_ROWS, 128),
-        path_gain,
+        jnp.stack((path_delay, path_angle, path_gain[0], path_gain[1])).reshape(4, PATH_ROWS, 128),
     )
     over, table, raw = call(
         transmit_kernel,
@@ -503,6 +489,7 @@
         [
             pltpu.SMEM((LINKS // 128, 128), i32),
             pltpu.VMEM((USERS * 8, 128), f32),
+            *SEED_SCRATCH,
             *SEED_SCRATCH,
             pltpu.SemaphoreType.DMA,
         ],

time: 50.3 us -> 49.2 us (0.978)
  Pallas kernels: 48.4 us -> 46.7 us
  local copies, waits for them, and re-layouts: 1.66 us -> 2.24 us
    pallas_call x1, Pallas kernels: 23 us -> 22.1 us  [shards(): call(deliver_kernel, 'deliver', 16, jax.ShapeDtypeStruct((CELLS, 8, 128),...]
    another operation x0 -> x1, local copies, waits for them, and re-layouts: none -> 0.94 us  [shards(): jnp.stack((path_delay, path_angle, path_gain[0], path_gain[1]))]
    pallas_call x1, Pallas kernels: 6.04 us -> 5.31 us  [shards(): call(transmit_kernel, 'transmit', 24, (jax.ShapeDtypeStruct((CELLS, 8, 12...]
    unnamed x9 -> x17, local copies, waits for them, and re-layouts: 1.66 us -> 1.3 us
where the time goes in v5:
time: 49.2 us; the launch traced here: 49.1 us
  Pallas kernels  46.7 us (95%)
  local copies, waits for them, and re-layouts  2.24 us (5%)
    pallas_call x1, Pallas kernels, shards(): call(deliver_kernel, 'deliver', 16, jax.ShapeDtypeStruct((CELLS, 8, 128),...  22.1 us
    pallas_call x1, Pallas kernels, shards(): call(receive_kernel, 'receive', 24, jax.ShapeDtypeStruct((USERS, 2, FRAME...  19.3 us
    pallas_call x1, Pallas kernels, shards(): call(transmit_kernel, 'transmit', 24, (jax.ShapeDtypeStruct((CELLS, 8, 12...  5.31 us
    unnamed x17, local copies, waits for them, and re-layouts  1.3 us

profile of v5, /device:TPU:1, one launch (start us, length us, event | category | flops | bytes accessed | tf_op | source)
XLA Modules:
  0.0 49.1 jit_solution(6180909240577845164)
XLA Ops:
  0.0 0.0 copy-start.6
  0.0 0.0 copy-start.7
  0.0 0.9 %stack.14 = f32[2,65,128]{2,1,0:T(8,128)S(1)} reshape(f32[2,8320]{1,0:T(2,128)} %param.11) | data formatting | bytes 133120 | tf_op jit(solution)/shard_map/stack | solution.py:477
  0.9 0.0 copy-done.6
  1.0 0.0 copy-done.7
  1.0 0.0 copy-start.2
  1.0 0.0 copy-start.3
  1.0 0.0 copy-start.4
  1.0 0.6 %copy-done.2 = s32[256]{0:T(256)S(1)} copy-done((s32[256]{0:T(256)S(1)}, s32[256]{0:T(256)}, u32[]{:S(2)}) %copy-start.2) | copy-done | bytes 1048
  1.7 0.0 copy-done.3
  1.7 0.0 copy-done.4
  1.7 0.0 copy-start
  1.7 0.0 copy-start.1
  1.7 0.0 copy-start.5
  1.7 22.1 %deliver.1.got = f32[128,8,128]{2,1,0:T(8,128)S(1)} custom-call(s32[256]{0:T(256)S(1)} %copy-done.2, s32[256]{0:T(256)S(1)} %copy-done.3, s32[256]{0:T(256)S(1)} %copy-done.4, f32[4,65,128]{2,1,0:T(8,128)S(1)} %pad_maximum_fusion.fields), custom_call_target="tpu_custom_call" | custom-call | tf_op jit(solution)/shard_map/deliver/pallas_call | solution.py:460
  23.8 0.0 copy-done
  23.8 0.0 copy-done.1
  23.8 0.0 copy-done.5
  23.8 5.3 %transmit.1 = (f32[128,8,128]{2,1,0:T(8,128)S(1)}, s32[2,128]{1,0:T(2,128)S(1)}, f32[32,64,128]{2,1,0:T(8,128)S(1)}) custom-call(s32[32]{0:T(128)S(1)} %copy-done.5, s32[8,32]{1,0:T(8,128)S(1)} %copy-done, f32[128,8,128]{2,1,0:T(8,128)S(1)} %deliver.1.got, bf16[32,2,128]{2,1,0:T(2,128)(2,1)S(1)} %copy-done.1), custom_call_target="tpu_custom_call" | custom-call | tf_op jit(solution)/shard_map/transmit/pallas_call | solution.py:479
  29.1 19.3 %receive.1 = f32[32,2,128]{2,1,0:T(2,128)S(1)} custom-call(s32[8,32]{1,0:T(8,128)S(1)} %copy-done, s32[2,128]{1,0:T(2,128)S(1)} %get-tuple-element.8.table, f32[128,8,128]{2,1,0:T(8,128)S(1)} %deliver.1.got, f32[128,8,128]{2,1,0:T(8,128)S(1)} %get-tuple-element.9.over, f32[32,64,128]{2,1,0:T(8,128)S(1)} %get-tuple-element.10.raw), custom_call_target="tpu_custom_call" | custom-call | tf_op jit(solution)/shard_map/receive/pallas_call | solution.py:497
  48.5 0.6 %copy.11 = f32[32,2,128]{2,1,0:T(2,128)} copy(f32[32,2,128]{2,1,0:T(2,128)S(1)} %receive.1) | data formatting | bytes 65536
  (1 shorter events, 0.0 us)
Async XLA Ops:
  0.0 0.9 %copy-start.6 = (f32[8320]{0:T(1024)S(1)}, f32[8320]{0:T(1024)}, u32[]{:S(2)}) copy-start(f32[8320]{0:T(1024)} %param.10) | copy-start | bytes 99844
  0.0 1.0 %copy-start.7 = (f32[8320]{0:T(1024)S(1)}, f32[8320]{0:T(1024)}, u32[]{:S(2)}) copy-start(f32[8320]{0:T(1024)} %param.9) | copy-start | bytes 99844
  1.0 0.7 %copy-start.2 = (s32[256]{0:T(256)S(1)}, s32[256]{0:T(256)}, u32[]{:S(2)}) copy-start(s32[256]{0:T(256)} %counts.1) | copy-start | bytes 3076
  1.0 0.7 %copy-start.3 = (s32[256]{0:T(256)S(1)}, s32[256]{0:T(256)}, u32[]{:S(2)}) copy-start(s32[256]{0:T(256)} %offsets.1) | copy-start | bytes 3076
  1.0 0.7 %copy-start.4 = (s32[256]{0:T(256)S(1)}, s32[256]{0:T(256)}, u32[]{:S(2)}) copy-start(s32[256]{0:T(256)} %links.1) | copy-start | bytes 3076
  1.7 22.1 %copy-start = (s32[8,32]{1,0:T(8,128)S(1)}, s32[8,32]{1,0:T(8,128)}, u32[]{:S(2)}) copy-start(s32[8,32]{1,0:T(8,128)} %nearby.3) | copy-start | bytes 3076
  1.7 22.1 %copy-start.1 = (bf16[32,2,128]{2,1,0:T(2,128)(2,1)S(1)}, bf16[32,2,128]{2,1,0:T(2,128)(2,1)}, u32[]{:S(2)}) copy-start(bf16[32,2,128]{2,1,0:T(2,128)(2,1)} %symbols.1) | copy-start | bytes 49156
  1.7 22.1 %copy-start.5 = (s32[32]{0:T(128)S(1)}, s32[32]{0:T(128)}, u32[]{:S(2)}) copy-start(s32[32]{0:T(128)} %slots.1) | copy-start | bytes 388

commit v6 on v5

--- a/solution.py
+++ b/solution.py
@@ -123,8 +123,8 @@
             value = pltpu.roll(value, (base - s) & 127, 1)
             j = place - base
             message = jnp.where((j >= 0) & (j < cnt), value, message)
-            message = jnp.where(tag_place == 2 * k, tag.astype(jnp.float32), message)
-            message = jnp.where(tag_place == 2 * k + 1, cnt.astype(jnp.float32), message)
+            for n, number_sent in enumerate((tag, cnt, base)):
+                message = jnp.where(tag_place == 3 * k + n, number_sent.astype(jnp.float32), message)
             base = base + cnt
         sent[o] = message
         return carry
@@ -245,12 +245,12 @@
 ]
 
 
-def unpacked(code, got, over):
-    source = code >> 16
-    base = (code >> 8) & 255
-    cnt = code & 255
+def unpacked(code, load):
+    base = code & 255
+    cnt = (code >> 8) & 255
     lane = lanes((8, 128))
-    value = jnp.where(lane < base + cnt - 128, over[source], got[source])
+    message, overflow = load(code >> 16)
+    value = jnp.where(lane < base + cnt - 128, overflow, message)
     return jnp.where(lane < cnt, pltpu.roll(value, (0 - base) & 127, 1), 0.0)
 
 
@@ -262,24 +262,21 @@
     grp = lax.axis_index("grp")
     lane = lanes((8, 128))
     row = rows_of((8, 128))
-    is_tag = (lane >= TAG_LANE) & (lane < TAG_LANE + 8) & (lax.rem(lane, 2) == 0)
-    link = (lane + 1).astype(jnp.float32)
-    found = [jnp.zeros((8, 128), jnp.float32) for _ in range(LINKS // 128)]
+    is_tag = (lane >= TAG_LANE) & (lane < TAG_LANE + 12)
+    link = lane + 1
+    found = [jnp.zeros((8, 128), jnp.int32) for _ in range(LINKS // 128)]
     for c in range(CELLS // 8):
-        extra = got[8 * c : 8 * c + 8, 4, :]
-        for f in range(4):
-            over[8 * c : 8 * c + 8, f, :] = extra if f == 0 else pltpu.roll(extra, 128 - 2 * f, 1)
-        cnt = jnp.where(is_tag, pltpu.roll(extra, 127, 1), 0.0)
-        base = pltpu.roll(cnt, 2, 1) + pltpu.roll(cnt, 4, 1) + pltpu.roll(cnt, 6, 1)
-        code = (8 * c + row).astype(jnp.float32) * 65536.0 + base * 256.0 + cnt
+        extra = got[pl.ds(64 * c + 4, 8, stride=8), :]
+        number = jnp.where(is_tag, extra, 0.0).astype(jnp.int32)
+        number = number + (pltpu.roll(number, 126, 1) << 9) + (pltpu.roll(number, 127, 1) << 17)
         for k in range(4):
-            at = TAG_LANE + 2 * k
-            tags = jnp.broadcast_to(extra[:, at : at + 1], (8, 128))
-            codes = jnp.broadcast_to(code[:, at : at + 1], (8, 128))
+            at = TAG_LANE + 3 * k
+            value = jnp.broadcast_to(number[:, at : at + 1], (8, 128))
+            code = (value >> 9) + ((8 * c + row) << 16)
             for h in range(LINKS // 128):
-                found[h] = found[h] + jnp.where(tags == link + 128.0 * h, codes, 0.0)
+                found[h] = found[h] + jnp.where((value & 511) == link + 128 * h, code, 0)
     for h in range(LINKS // 128):
-        table[h : h + 1, :] = jnp.sum(found[h], axis=0, keepdims=True).astype(jnp.int32)
+        table[h : h + 1, :] = jnp.sum(found[h], axis=0, keepdims=True)
     copy = pltpu.make_async_copy(table, table_s, sem)
     copy.start()
 
@@ -288,12 +285,20 @@
         return carry
 
     lax.fori_loop(0, CELL_SECTORS, clear, 0, unroll=4)
+    for c in range(CELLS // 8):
+        extra = got[pl.ds(64 * c + 4, 8, stride=8), :]
+        for f in range(4):
+            over[pl.ds(64 * c + f, 8, stride=8), :] = extra if f == 0 else pltpu.roll(extra, 128 - 2 * f, 1)
     copy.wait()
+
+    def load(source):
+        at = pl.ds(pl.multiple_of(8 * source, 8), 8)
+        return got[at, :], over[at, :]
 
     def serve(u, carry):
         g = u * NEARBY_COUNT + slots[u]
         code = table_s[g >> 7, g & 127]
-        serving[pl.ds(pl.multiple_of(8 * u, 8), 8), :] = unpacked(code, got, over)
+        serving[pl.ds(pl.multiple_of(8 * u, 8), 8), :] = unpacked(code, load)
         return carry
 
     lax.fori_loop(0, USERS, serve, 0, unroll=8)
@@ -370,7 +375,7 @@
         u = jnp.minimum(u, USERS - 1)
         for l in range(8):
             code = table[u // 16, lax.rem(u, 16) * 8 + l]
-            rows[8 * l : 8 * l + 8, :] = unpacked(code, got, over)
+            rows[8 * l : 8 * l + 8, :] = unpacked(code, lambda i: (got[i], over[i]))
 
     def prepare(rows, seeds):
         seeds_of([rows[pl.ds(f, 8, stride=8), :] for f in range(4)], grp, *seeds)
@@ -481,7 +486,7 @@
         "transmit",
         24,
         (
-            jax.ShapeDtypeStruct((CELLS, 8, 128), f32),
+            jax.ShapeDtypeStruct((CELLS * 8, 128), f32),
             jax.ShapeDtypeStruct((LINKS // 128, 128), i32),
             jax.ShapeDtypeStruct((CELL_SECTORS, RESP, 128), f32),
         ),
@@ -493,7 +498,7 @@
             *SEED_SCRATCH,
             pltpu.SemaphoreType.DMA,
         ],
-    )(serving_slot, nearby_sectors, got, symbols)
+    )(serving_slot, nearby_sectors, got.reshape(CELLS * 8, 128), symbols)
     return call(
         receive_kernel,
         "receive",
@@ -513,7 +518,7 @@
             pltpu.SemaphoreType.DMA((len(PIECES) + 1,)),
         ],
         remote=1,
-    )(nearby_sectors, table, got, over, raw)
+    )(nearby_sectors, table, got, over.reshape(CELLS, 8, 128), raw)
 
 
 def solution(mesh):

time: 49.2 us -> 47.6 us (0.967)
  Pallas kernels: 46.7 us -> 44.5 us
  local copies, waits for them, and re-layouts: 2.24 us -> 2.87 us
    pallas_call x1, Pallas kernels: 5.31 us -> 3 us  [shards(): call(transmit_kernel, 'transmit', 24, (jax.ShapeDtypeStruct((CELLS * 8, 1...]
    unnamed x17, local copies, waits for them, and re-layouts: 1.3 us -> 1.93 us
where the time goes in v6:
time: 47.6 us; the launch traced here: 47.5 us
  Pallas kernels  44.5 us (93%)
  local copies, waits for them, and re-layouts  2.87 us (6%)
    pallas_call x1, Pallas kernels, shards(): call(deliver_kernel, 'deliver', 16, jax.ShapeDtypeStruct((CELLS, 8, 128),...  22.1 us
    pallas_call x1, Pallas kernels, shards(): call(receive_kernel, 'receive', 24, jax.ShapeDtypeStruct((USERS, 2, FRAME...  19.4 us
    pallas_call x1, Pallas kernels, shards(): call(transmit_kernel, 'transmit', 24, (jax.ShapeDtypeStruct((CELLS * 8, 1...  3 us
    unnamed x17, local copies, waits for them, and re-layouts  1.93 us

profile of v6, /device:TPU:1, one launch (start us, length us, event | category | flops | bytes accessed | tf_op | source)
XLA Modules:
  0.0 47.5 jit_solution(12146648317080459993)
XLA Ops:
  0.0 0.0 copy-start.6
  0.0 0.0 copy-start.7
  0.0 0.9 %stack.14 = f32[2,65,128]{2,1,0:T(8,128)S(1)} reshape(f32[2,8320]{1,0:T(2,128)} %param.11) | data formatting | bytes 133120 | tf_op jit(solution)/shard_map/stack | solution.py:482
  0.9 0.0 copy-done.6
  1.0 0.0 copy-done.7
  1.0 0.0 copy-start.2
  1.0 0.0 copy-start.3
  1.0 0.0 copy-start.4
  1.0 0.6 %copy-done.2 = s32[256]{0:T(256)S(1)} copy-done((s32[256]{0:T(256)S(1)}, s32[256]{0:T(256)}, u32[]{:S(2)}) %copy-start.2) | copy-done | bytes 1048
  1.7 0.0 copy-done.3
  1.7 0.0 copy-done.4
  1.7 0.0 copy-start
  1.7 0.0 copy-start.1
  1.7 22.1 %deliver.1.got = f32[128,8,128]{2,1,0:T(8,128)S(1)} custom-call(s32[256]{0:T(256)S(1)} %copy-done.2, s32[256]{0:T(256)S(1)} %copy-done.3, s32[256]{0:T(256)S(1)} %copy-done.4, f32[4,65,128]{2,1,0:T(8,128)S(1)} %pad_maximum_fusion.fields), custom_call_target="tpu_custom_call" | custom-call | tf_op jit(solution)/shard_map/deliver/pallas_call | solution.py:465
  23.8 0.0 copy-start.5
  23.8 0.0 copy-done
  23.8 0.0 copy-done.1
  23.8 0.6 %copy-done.5 = s32[32]{0:T(128)S(1)} copy-done((s32[32]{0:T(128)S(1)}, s32[32]{0:T(128)}, u32[]{:S(2)}) %copy-start.5) | copy-done | bytes 152
  24.4 3.0 %transmit.1 = (f32[1024,128]{1,0:T(8,128)S(1)}, s32[2,128]{1,0:T(2,128)S(1)}, f32[32,64,128]{2,1,0:T(8,128)S(1)}) custom-call(s32[32]{0:T(128)S(1)} %copy-done.5, s32[8,32]{1,0:T(8,128)S(1)} %copy-done, f32[1024,128]{1,0:T(8,128)S(1)} %bitcast.4, bf16[32,2,128]{2,1,0:T(2,128)(2,1)S(1)} %copy-done.1), custom_call_target="tpu_custom_call" | custom-call | tf_op jit(solution)/shard_map/transmit/pallas_call | solution.py:484
  27.5 19.4 %receive.1 = f32[32,2,128]{2,1,0:T(2,128)S(1)} custom-call(s32[8,32]{1,0:T(8,128)S(1)} %copy-done, s32[2,128]{1,0:T(2,128)S(1)} %get-tuple-element.8.table, f32[128,8,128]{2,1,0:T(8,128)S(1)} %deliver.1.got, f32[128,8,128]{2,1,0:T(8,128)S(1)} %bitcast.5, f32[32,64,128]{2,1,0:T(8,128)S(1)} %get-tuple-element.10.raw), custom_call_target="tpu_custom_call" | custom-call | tf_op jit(solution)/shard_map/receive/pallas_call | solution.py:502
  46.8 0.6 %copy.11 = f32[32,2,128]{2,1,0:T(2,128)} copy(f32[32,2,128]{2,1,0:T(2,128)S(1)} %receive.1) | data formatting | bytes 65536
  (1 shorter events, 0.0 us)
Async XLA Ops:
  0.0 0.9 %copy-start.6 = (f32[8320]{0:T(1024)S(1)}, f32[8320]{0:T(1024)}, u32[]{:S(2)}) copy-start(f32[8320]{0:T(1024)} %param.10) | copy-start | bytes 99844
  0.0 1.0 %copy-start.7 = (f32[8320]{0:T(1024)S(1)}, f32[8320]{0:T(1024)}, u32[]{:S(2)}) copy-start(f32[8320]{0:T(1024)} %param.9) | copy-start | bytes 99844
  1.0 0.7 %copy-start.2 = (s32[256]{0:T(256)S(1)}, s32[256]{0:T(256)}, u32[]{:S(2)}) copy-start(s32[256]{0:T(256)} %counts.1) | copy-start | bytes 3076
  1.0 0.7 %copy-start.3 = (s32[256]{0:T(256)S(1)}, s32[256]{0:T(256)}, u32[]{:S(2)}) copy-start(s32[256]{0:T(256)} %offsets.1) | copy-start | bytes 3076
  1.0 0.7 %copy-start.4 = (s32[256]{0:T(256)S(1)}, s32[256]{0:T(256)}, u32[]{:S(2)}) copy-start(s32[256]{0:T(256)} %links.1) | copy-start | bytes 3076
  1.7 22.1 %copy-start = (s32[8,32]{1,0:T(8,128)S(1)}, s32[8,32]{1,0:T(8,128)}, u32[]{:S(2)}) copy-start(s32[8,32]{1,0:T(8,128)} %nearby.3) | copy-start | bytes 3076
  1.7 22.1 %copy-start.1 = (bf16[32,2,128]{2,1,0:T(2,128)(2,1)S(1)}, bf16[32,2,128]{2,1,0:T(2,128)(2,1)}, u32[]{:S(2)}) copy-start(bf16[32,2,128]{2,1,0:T(2,128)(2,1)} %symbols.1) | copy-start | bytes 49156
  23.8 0.7 %copy-start.5 = (s32[32]{0:T(128)S(1)}, s32[32]{0:T(128)}, u32[]{:S(2)}) copy-start(s32[32]{0:T(128)} %slots.1) | copy-start | bytes 388

commit v7 on v6

--- a/solution.py
+++ b/solution.py
@@ -56,7 +56,7 @@
 
 
 def deliver_kernel(
-    counts, offsets, links, fields, got, store, sent, begins, sems
+    counts, offsets, links, _slots, fields, got, store, sent, begins, sems
 ):
     me = lax.axis_index("cell")
     grp = lax.axis_index("grp")
@@ -70,7 +70,11 @@
         pl.semaphore_signal(barrier, inc=1, device_id={"cell": other}, device_id_type=MESH)
         return carry
 
-    lax.fori_loop(1 - grp, HALF, greet, 0)
+    @pl.when(grp == 1)
+    def _():
+        greet(0, 0)
+
+    lax.fori_loop(1, HALF, greet, 0, unroll=9)
 
     def narrow(_, carry):
         low, top = carry
@@ -352,7 +356,7 @@
             near[REACH + s] = jnp.concatenate([real * scale, imag * scale], axis=0).astype(jnp.bfloat16)
             return carry
 
-        lax.fori_loop(begin, begin + PIECE, normalise, 0, unroll=4)
+        lax.fori_loop(begin, begin + PIECE, normalise, 0, unroll=8)
         if n == 0:
             pl.semaphore_wait(barrier, 3)
         to_left = begin < CELL_SECTORS - REACH
@@ -418,7 +422,7 @@
         )
         return carry
 
-    lax.fori_loop(0, USERS, combine, 0)
+    lax.fori_loop(0, USERS, combine, 0, unroll=4)
     swap = pltpu.make_async_remote_copy(
         src_ref=part,
         dst_ref=other,
@@ -467,7 +471,7 @@
         "deliver",
         16,
         jax.ShapeDtypeStruct((CELLS, 8, 128), f32),
-        [SMEM, SMEM, SMEM, VMEM],
+        [SMEM, SMEM, SMEM, SMEM, VMEM],
         [
             pltpu.VMEM((PATH_ROWS + 1, 8, 128), f32),
             pltpu.VMEM((HALF, 8, 128), f32),
@@ -479,6 +483,7 @@
         slot_counts,
         slot_offsets,
         ray_link,
+        serving_slot,
         jnp.stack((path_delay, path_angle, path_gain[0], path_gain[1])).reshape(4, PATH_ROWS, 128),
     )
     over, table, raw = call(

time: 47.6 us -> 46.3 us (0.973)
  Pallas kernels: 44.5 us -> 43.8 us
  local copies, waits for them, and re-layouts: 2.87 us -> 2.25 us
    unnamed x17, local copies, waits for them, and re-layouts: 1.93 us -> 1.31 us
where the time goes in v7:
time: 46.3 us; the launch traced here: 46.2 us
  Pallas kernels  43.8 us (95%)
  local copies, waits for them, and re-layouts  2.25 us (5%)
    pallas_call x1, Pallas kernels, shards(): call(deliver_kernel, 'deliver', 16, jax.ShapeDtypeStruct((CELLS, 8, 128),...  21.8 us
    pallas_call x1, Pallas kernels, shards(): call(receive_kernel, 'receive', 24, jax.ShapeDtypeStruct((USERS, 2, FRAME...  19 us
    pallas_call x1, Pallas kernels, shards(): call(transmit_kernel, 'transmit', 24, (jax.ShapeDtypeStruct((CELLS * 8, 1...  3 us
    unnamed x17, local copies, waits for them, and re-layouts  1.31 us
    another operation x1, local copies, waits for them, and re-layouts, shards(): jnp.stack((path_delay, path_angle, path_gain[0], path_gain[1]))  0.94 us

profile of v7, /device:TPU:1, one launch (start us, length us, event | category | flops | bytes accessed | tf_op | source)
XLA Modules:
  0.0 46.2 jit_solution(9306327437964039826)
XLA Ops:
  0.0 0.0 copy-start.6
  0.0 0.0 copy-start.7
  0.0 0.9 %stack.14 = f32[2,65,128]{2,1,0:T(8,128)S(1)} reshape(f32[2,8320]{1,0:T(2,128)} %param.11) | data formatting | bytes 133120 | tf_op jit(solution)/shard_map/stack | solution.py:487
  0.9 0.0 copy-done.6
  1.0 0.0 copy-done.7
  1.0 0.0 copy-start.2
  1.0 0.0 copy-start.3
  1.0 0.0 copy-start.4
  1.0 0.0 copy-start.5
  1.0 0.6 %copy-done.2 = s32[32]{0:T(128)S(1)} copy-done((s32[32]{0:T(128)S(1)}, s32[32]{0:T(128)}, u32[]{:S(2)}) %copy-start.2) | copy-done | bytes 152
  1.6 0.0 copy-done.3
  1.7 0.0 copy-done.4
  1.7 0.0 copy-done.5
  1.7 0.0 copy-start
  1.7 0.0 copy-start.1
  1.7 21.8 %deliver.1.got = f32[128,8,128]{2,1,0:T(8,128)S(1)} custom-call(s32[256]{0:T(256)S(1)} %copy-done.3, s32[256]{0:T(256)S(1)} %copy-done.4, s32[256]{0:T(256)S(1)} %copy-done.5, s32[32]{0:T(128)S(1)} %copy-done.2, f32[4,65,128]{2,1,0:T(8,128)S(1)} %pad_maximum_fusion.fields), custom_call_target="tpu_custom_call" | custom-call | tf_op jit(solution)/shard_map/deliver/pallas_call | solution.py:469
  23.5 0.0 copy-done
  23.5 0.0 copy-done.1
  23.5 3.0 %transmit.1 = (f32[1024,128]{1,0:T(8,128)S(1)}, s32[2,128]{1,0:T(2,128)S(1)}, f32[32,64,128]{2,1,0:T(8,128)S(1)}) custom-call(s32[32]{0:T(128)S(1)} %copy-done.2, s32[8,32]{1,0:T(8,128)S(1)} %copy-done, f32[1024,128]{1,0:T(8,128)S(1)} %bitcast.4, bf16[32,2,128]{2,1,0:T(2,128)(2,1)S(1)} %copy-done.1), custom_call_target="tpu_custom_call" | custom-call | tf_op jit(solution)/shard_map/transmit/pallas_call | solution.py:489
  26.5 19.0 %receive.1 = f32[32,2,128]{2,1,0:T(2,128)S(1)} custom-call(s32[8,32]{1,0:T(8,128)S(1)} %copy-done, s32[2,128]{1,0:T(2,128)S(1)} %get-tuple-element.8.table, f32[128,8,128]{2,1,0:T(8,128)S(1)} %deliver.1.got, f32[128,8,128]{2,1,0:T(8,128)S(1)} %bitcast.5, f32[32,64,128]{2,1,0:T(8,128)S(1)} %get-tuple-element.10.raw), custom_call_target="tpu_custom_call" | custom-call | tf_op jit(solution)/shard_map/receive/pallas_call | solution.py:507
  45.5 0.6 %copy.11 = f32[32,2,128]{2,1,0:T(2,128)} copy(f32[32,2,128]{2,1,0:T(2,128)S(1)} %receive.1) | data formatting | bytes 65536
  (1 shorter events, 0.0 us)
Async XLA Ops:
  0.0 0.9 %copy-start.6 = (f32[8320]{0:T(1024)S(1)}, f32[8320]{0:T(1024)}, u32[]{:S(2)}) copy-start(f32[8320]{0:T(1024)} %param.10) | copy-start | bytes 99844
  0.0 1.0 %copy-start.7 = (f32[8320]{0:T(1024)S(1)}, f32[8320]{0:T(1024)}, u32[]{:S(2)}) copy-start(f32[8320]{0:T(1024)} %param.9) | copy-start | bytes 99844
  1.0 0.7 %copy-start.2 = (s32[32]{0:T(128)S(1)}, s32[32]{0:T(128)}, u32[]{:S(2)}) copy-start(s32[32]{0:T(128)} %slots.1) | copy-start | bytes 388
  1.0 0.7 %copy-start.3 = (s32[256]{0:T(256)S(1)}, s32[256]{0:T(256)}, u32[]{:S(2)}) copy-start(s32[256]{0:T(256)} %counts.1) | copy-start | bytes 3076
  1.0 0.7 %copy-start.4 = (s32[256]{0:T(256)S(1)}, s32[256]{0:T(256)}, u32[]{:S(2)}) copy-start(s32[256]{0:T(256)} %offsets.1) | copy-start | bytes 3076
  1.0 0.7 %copy-start.5 = (s32[256]{0:T(256)S(1)}, s32[256]{0:T(256)}, u32[]{:S(2)}) copy-start(s32[256]{0:T(256)} %links.1) | copy-start | bytes 3076
  1.7 21.8 %copy-start = (s32[8,32]{1,0:T(8,128)S(1)}, s32[8,32]{1,0:T(8,128)}, u32[]{:S(2)}) copy-start(s32[8,32]{1,0:T(8,128)} %nearby.3) | copy-start | bytes 3076
  1.7 21.8 %copy-start.1 = (bf16[32,2,128]{2,1,0:T(2,128)(2,1)S(1)}, bf16[32,2,128]{2,1,0:T(2,128)(2,1)}, u32[]{:S(2)}) copy-start(bf16[32,2,128]{2,1,0:T(2,128)(2,1)} %symbols.1) | copy-start | bytes 49156

commit v8 on v7

--- a/solution.py
+++ b/solution.py
@@ -56,12 +56,19 @@
 
 
 def deliver_kernel(
-    counts, offsets, links, _slots, fields, got, store, sent, begins, sems
+    counts_in, offsets_in, links_in, _slots, fields, got,
+    counts, offsets, links, store, sent, begins, load_sems, sems
 ):
     me = lax.axis_index("cell")
     grp = lax.axis_index("grp")
     start = my_half() * HALF
     sibling = {"grp": 1 - grp}
+    loads = [
+        pltpu.make_async_copy(src, dst, load_sems.at[n])
+        for n, (src, dst) in enumerate(((counts_in, counts), (offsets_in, offsets), (links_in, links)))
+    ]
+    for copy in loads:
+        copy.start()
     barrier = pltpu.get_barrier_semaphore()
     pl.semaphore_signal(barrier, inc=1, device_id=sibling, device_id_type=MESH)
 
@@ -75,6 +82,9 @@
         greet(0, 0)
 
     lax.fori_loop(1, HALF, greet, 0, unroll=9)
+
+    for copy in loads:
+        copy.wait()
 
     def narrow(_, carry):
         low, top = carry
@@ -147,8 +157,8 @@
     pl.semaphore_wait(barrier, HALF + grp)
     wire = pl.ds(0, WIRE_ROWS)
 
-    def send(d, carry):
-        near = lax.rem(me + d, HALF)
+    def send(hops, q, carry):
+        near = lax.rem(me + 8 * q + hops, HALF)
         pltpu.make_async_remote_copy(
             src_ref=sent.at[near, wire],
             dst_ref=got.at[me, wire],
@@ -159,7 +169,9 @@
         ).start()
         return carry
 
-    lax.fori_loop(1 - grp, HALF, send, 0)
+    for hops in (4, 3, 5, 2, 6, 1, 7):
+        lax.fori_loop(0, HALF // 8, functools.partial(send, hops), 0, unroll=4)
+    lax.fori_loop(1 - grp, HALF // 8, functools.partial(send, 0), 0)
 
     for g in range(2):
 
@@ -438,6 +450,7 @@
 
 VMEM = pl.BlockSpec(memory_space=pltpu.VMEM)
 SMEM = pl.BlockSpec(memory_space=pltpu.SMEM)
+ANY = pl.BlockSpec(memory_space=pl.ANY)
 
 
 def call(kernel, name, mib, out_shape, in_specs, scratch, remote=None):
@@ -471,11 +484,15 @@
         "deliver",
         16,
         jax.ShapeDtypeStruct((CELLS, 8, 128), f32),
-        [SMEM, SMEM, SMEM, SMEM, VMEM],
+        [ANY, ANY, ANY, ANY, VMEM],
         [
+            pltpu.SMEM((SLOTS,), i32),
+            pltpu.SMEM((SLOTS,), i32),
+            pltpu.SMEM((SLOTS,), i32),
             pltpu.VMEM((PATH_ROWS + 1, 8, 128), f32),
             pltpu.VMEM((HALF, 8, 128), f32),
             pltpu.SMEM((HALF + 1,), i32),
+            pltpu.SemaphoreType.DMA((3,)),
             pltpu.SemaphoreType.DMA((4,)),
         ],
         remote=0,

time: 46.3 us -> 44.8 us (0.968)
  Pallas kernels: 43.8 us -> 42.3 us
    pallas_call x1, Pallas kernels: 21.8 us -> 20.4 us  [shards(): call(deliver_kernel, 'deliver', 16, jax.ShapeDtypeStruct((CELLS, 8, 128),...]
where the time goes in v8:
time: 44.8 us; the launch traced here: 44.7 us
  Pallas kernels  42.3 us (94%)
  local copies, waits for them, and re-layouts  2.25 us (5%)
    pallas_call x1, Pallas kernels, shards(): call(deliver_kernel, 'deliver', 16, jax.ShapeDtypeStruct((CELLS, 8, 128),...  20.4 us
    pallas_call x1, Pallas kernels, shards(): call(receive_kernel, 'receive', 24, jax.ShapeDtypeStruct((USERS, 2, FRAME...  18.9 us
    pallas_call x1, Pallas kernels, shards(): call(transmit_kernel, 'transmit', 24, (jax.ShapeDtypeStruct((CELLS * 8, 1...  3 us
    unnamed x17, local copies, waits for them, and re-layouts  1.31 us
    another operation x1, local copies, waits for them, and re-layouts, shards(): jnp.stack((path_delay, path_angle, path_gain[0], path_gain[1]))  0.94 us

profile of v8, /device:TPU:1, one launch (start us, length us, event | category | flops | bytes accessed | tf_op | source)
XLA Modules:
  0.0 44.7 jit_solution(17563403677242361710)
XLA Ops:
  0.0 0.0 copy-start.6
  0.0 0.0 copy-start.7
  0.0 0.9 %stack.14 = f32[2,65,128]{2,1,0:T(8,128)S(1)} reshape(f32[2,8320]{1,0:T(2,128)} %param.11) | data formatting | bytes 133120 | tf_op jit(solution)/shard_map/stack | solution.py:504
  0.9 0.0 copy-done.6
  1.0 0.0 copy-done.7
  1.0 0.0 copy-start.2
  1.0 0.0 copy-start.3
  1.0 0.0 copy-start.4
  1.0 0.0 copy-start.5
  1.0 0.6 %copy-done.2 = s32[32]{0:T(128)S(1)} copy-done((s32[32]{0:T(128)S(1)}, s32[32]{0:T(128)}, u32[]{:S(2)}) %copy-start.2) | copy-done | bytes 152
  1.6 0.0 copy-done.3
  1.7 0.0 copy-done.4
  1.7 0.0 copy-done.5
  1.7 0.0 copy-start
  1.7 0.0 copy-start.1
  1.7 20.4 %deliver.1.got = f32[128,8,128]{2,1,0:T(8,128)S(1)} custom-call(s32[256]{0:T(256)S(1)} %copy-done.3, s32[256]{0:T(256)S(1)} %copy-done.4, s32[256]{0:T(256)S(1)} %copy-done.5, s32[32]{0:T(128)S(1)} %copy-done.2, f32[4,65,128]{2,1,0:T(8,128)S(1)} %pad_maximum_fusion.fields), custom_call_target="tpu_custom_call" | custom-call | tf_op jit(solution)/shard_map/deliver/pallas_call | solution.py:482
  22.2 0.0 copy-done
  22.2 0.0 copy-done.1
  22.2 3.0 %transmit.1 = (f32[1024,128]{1,0:T(8,128)S(1)}, s32[2,128]{1,0:T(2,128)S(1)}, f32[32,64,128]{2,1,0:T(8,128)S(1)}) custom-call(s32[32]{0:T(128)S(1)} %copy-done.2, s32[8,32]{1,0:T(8,128)S(1)} %copy-done, f32[1024,128]{1,0:T(8,128)S(1)} %bitcast.4, bf16[32,2,128]{2,1,0:T(2,128)(2,1)S(1)} %copy-done.1), custom_call_target="tpu_custom_call" | custom-call | tf_op jit(solution)/shard_map/transmit/pallas_call | solution.py:506
  25.2 18.9 %receive.1 = f32[32,2,128]{2,1,0:T(2,128)S(1)} custom-call(s32[8,32]{1,0:T(8,128)S(1)} %copy-done, s32[2,128]{1,0:T(2,128)S(1)} %get-tuple-element.8.table, f32[128,8,128]{2,1,0:T(8,128)S(1)} %deliver.1.got, f32[128,8,128]{2,1,0:T(8,128)S(1)} %bitcast.5, f32[32,64,128]{2,1,0:T(8,128)S(1)} %get-tuple-element.10.raw), custom_call_target="tpu_custom_call" | custom-call | tf_op jit(solution)/shard_map/receive/pallas_call | solution.py:524
  44.1 0.6 %copy.11 = f32[32,2,128]{2,1,0:T(2,128)} copy(f32[32,2,128]{2,1,0:T(2,128)S(1)} %receive.1) | data formatting | bytes 65536
  (1 shorter events, 0.0 us)
Async XLA Ops:
  0.0 0.9 %copy-start.6 = (f32[8320]{0:T(1024)S(1)}, f32[8320]{0:T(1024)}, u32[]{:S(2)}) copy-start(f32[8320]{0:T(1024)} %param.10) | copy-start | bytes 99844
  0.0 1.0 %copy-start.7 = (f32[8320]{0:T(1024)S(1)}, f32[8320]{0:T(1024)}, u32[]{:S(2)}) copy-start(f32[8320]{0:T(1024)} %param.9) | copy-start | bytes 99844
  1.0 0.7 %copy-start.2 = (s32[32]{0:T(128)S(1)}, s32[32]{0:T(128)}, u32[]{:S(2)}) copy-start(s32[32]{0:T(128)} %slots.1) | copy-start | bytes 388
  1.0 0.7 %copy-start.3 = (s32[256]{0:T(256)S(1)}, s32[256]{0:T(256)}, u32[]{:S(2)}) copy-start(s32[256]{0:T(256)} %counts_in.1) | copy-start | bytes 3076
  1.0 0.7 %copy-start.4 = (s32[256]{0:T(256)S(1)}, s32[256]{0:T(256)}, u32[]{:S(2)}) copy-start(s32[256]{0:T(256)} %offsets_in.1) | copy-start | bytes 3076
  1.0 0.7 %copy-start.5 = (s32[256]{0:T(256)S(1)}, s32[256]{0:T(256)}, u32[]{:S(2)}) copy-start(s32[256]{0:T(256)} %links_in.1) | copy-start | bytes 3076
  1.7 20.5 %copy-start = (s32[8,32]{1,0:T(8,128)S(1)}, s32[8,32]{1,0:T(8,128)}, u32[]{:S(2)}) copy-start(s32[8,32]{1,0:T(8,128)} %nearby.3) | copy-start | bytes 3076
  1.7 20.5 %copy-start.1 = (bf16[32,2,128]{2,1,0:T(2,128)(2,1)S(1)}, bf16[32,2,128]{2,1,0:T(2,128)(2,1)}, u32[]{:S(2)}) copy-start(bf16[32,2,128]{2,1,0:T(2,128)(2,1)} %symbols.1) | copy-start | bytes 49156

commit v9 on v8

--- a/solution.py
+++ b/solution.py
@@ -342,8 +342,8 @@
             raw[sector] = raw[sector] + part
 
 
-PIECE = 8
-PIECES = (0, 16, 8, 24)
+PIECE = REACH
+PIECES = (0, 16)
 
 
 def receive_kernel(

time: 44.8 us -> 44.6 us (level)
  no operation moved by 1% of the time
where the time goes in v9:
time: 44.6 us; the launch traced here: 44.4 us
  Pallas kernels  42.1 us (94%)
  local copies, waits for them, and re-layouts  2.25 us (5%)
    pallas_call x1, Pallas kernels, shards(): call(deliver_kernel, 'deliver', 16, jax.ShapeDtypeStruct((CELLS, 8, 128),...  20.4 us
    pallas_call x1, Pallas kernels, shards(): call(receive_kernel, 'receive', 24, jax.ShapeDtypeStruct((USERS, 2, FRAME...  18.6 us
    pallas_call x1, Pallas kernels, shards(): call(transmit_kernel, 'transmit', 24, (jax.ShapeDtypeStruct((CELLS * 8, 1...  3 us
    unnamed x17, local copies, waits for them, and re-layouts  1.31 us
    another operation x1, local copies, waits for them, and re-layouts, shards(): jnp.stack((path_delay, path_angle, path_gain[0], path_gain[1]))  0.94 us

profile of v9, /device:TPU:1, one launch (start us, length us, event | category | flops | bytes accessed | tf_op | source)
XLA Modules:
  0.0 44.4 jit_solution(13634031489962156396)
XLA Ops:
  0.0 0.0 copy-start.6
  0.0 0.0 copy-start.7
  0.0 0.9 %stack.14 = f32[2,65,128]{2,1,0:T(8,128)S(1)} reshape(f32[2,8320]{1,0:T(2,128)} %param.11) | data formatting | bytes 133120 | tf_op jit(solution)/shard_map/stack | solution.py:504
  0.9 0.0 copy-done.6
  1.0 0.0 copy-done.7
  1.0 0.0 copy-start.2
  1.0 0.0 copy-start.3
  1.0 0.0 copy-start.4
  1.0 0.0 copy-start.5
  1.0 0.6 %copy-done.2 = s32[32]{0:T(128)S(1)} copy-done((s32[32]{0:T(128)S(1)}, s32[32]{0:T(128)}, u32[]{:S(2)}) %copy-start.2) | copy-done | bytes 152
  1.6 0.0 copy-done.3
  1.7 0.0 copy-done.4
  1.7 0.0 copy-done.5
  1.7 0.0 copy-start
  1.7 0.0 copy-start.1
  1.7 20.4 %deliver.1.got = f32[128,8,128]{2,1,0:T(8,128)S(1)} custom-call(s32[256]{0:T(256)S(1)} %copy-done.3, s32[256]{0:T(256)S(1)} %copy-done.4, s32[256]{0:T(256)S(1)} %copy-done.5, s32[32]{0:T(128)S(1)} %copy-done.2, f32[4,65,128]{2,1,0:T(8,128)S(1)} %pad_maximum_fusion.fields), custom_call_target="tpu_custom_call" | custom-call | tf_op jit(solution)/shard_map/deliver/pallas_call | solution.py:482
  22.2 0.0 copy-done
  22.2 0.0 copy-done.1
  22.2 3.0 %transmit.1 = (f32[1024,128]{1,0:T(8,128)S(1)}, s32[2,128]{1,0:T(2,128)S(1)}, f32[32,64,128]{2,1,0:T(8,128)S(1)}) custom-call(s32[32]{0:T(128)S(1)} %copy-done.2, s32[8,32]{1,0:T(8,128)S(1)} %copy-done, f32[1024,128]{1,0:T(8,128)S(1)} %bitcast.4, bf16[32,2,128]{2,1,0:T(2,128)(2,1)S(1)} %copy-done.1), custom_call_target="tpu_custom_call" | custom-call | tf_op jit(solution)/shard_map/transmit/pallas_call | solution.py:506
  25.2 18.6 %receive.1 = f32[32,2,128]{2,1,0:T(2,128)S(1)} custom-call(s32[8,32]{1,0:T(8,128)S(1)} %copy-done, s32[2,128]{1,0:T(2,128)S(1)} %get-tuple-element.8.table, f32[128,8,128]{2,1,0:T(8,128)S(1)} %deliver.1.got, f32[128,8,128]{2,1,0:T(8,128)S(1)} %bitcast.5, f32[32,64,128]{2,1,0:T(8,128)S(1)} %get-tuple-element.10.raw), custom_call_target="tpu_custom_call" | custom-call | tf_op jit(solution)/shard_map/receive/pallas_call | solution.py:524
  43.8 0.6 %copy.11 = f32[32,2,128]{2,1,0:T(2,128)} copy(f32[32,2,128]{2,1,0:T(2,128)S(1)} %receive.1) | data formatting | bytes 65536
  (1 shorter events, 0.0 us)
Async XLA Ops:
  0.0 0.9 %copy-start.6 = (f32[8320]{0:T(1024)S(1)}, f32[8320]{0:T(1024)}, u32[]{:S(2)}) copy-start(f32[8320]{0:T(1024)} %param.10) | copy-start | bytes 99844
  0.0 1.0 %copy-start.7 = (f32[8320]{0:T(1024)S(1)}, f32[8320]{0:T(1024)}, u32[]{:S(2)}) copy-start(f32[8320]{0:T(1024)} %param.9) | copy-start | bytes 99844
  1.0 0.7 %copy-start.2 = (s32[32]{0:T(128)S(1)}, s32[32]{0:T(128)}, u32[]{:S(2)}) copy-start(s32[32]{0:T(128)} %slots.1) | copy-start | bytes 388
  1.0 0.7 %copy-start.3 = (s32[256]{0:T(256)S(1)}, s32[256]{0:T(256)}, u32[]{:S(2)}) copy-start(s32[256]{0:T(256)} %counts_in.1) | copy-start | bytes 3076
  1.0 0.7 %copy-start.4 = (s32[256]{0:T(256)S(1)}, s32[256]{0:T(256)}, u32[]{:S(2)}) copy-start(s32[256]{0:T(256)} %offsets_in.1) | copy-start | bytes 3076
  1.0 0.7 %copy-start.5 = (s32[256]{0:T(256)S(1)}, s32[256]{0:T(256)}, u32[]{:S(2)}) copy-start(s32[256]{0:T(256)} %links_in.1) | copy-start | bytes 3076
  1.7 20.5 %copy-start = (s32[8,32]{1,0:T(8,128)S(1)}, s32[8,32]{1,0:T(8,128)}, u32[]{:S(2)}) copy-start(s32[8,32]{1,0:T(8,128)} %nearby.3) | copy-start | bytes 3076
  1.7 20.5 %copy-start.1 = (bf16[32,2,128]{2,1,0:T(2,128)(2,1)S(1)}, bf16[32,2,128]{2,1,0:T(2,128)(2,1)}, u32[]{:S(2)}) copy-start(bf16[32,2,128]{2,1,0:T(2,128)(2,1)} %symbols.1) | copy-start | bytes 49156

commit v10 on v9

--- a/solution.py
+++ b/solution.py
@@ -173,21 +173,18 @@
         lax.fori_loop(0, HALF // 8, functools.partial(send, hops), 0, unroll=4)
     lax.fori_loop(1 - grp, HALF // 8, functools.partial(send, 0), 0)
 
+    def messages(number):
+        return pltpu.make_async_remote_copy(
+            src_ref=sent.at[pl.ds(0, number), wire],
+            dst_ref=got.at[pl.ds(start, number), wire],
+            send_sem=sems.at[0],
+            recv_sem=sems.at[1],
+            device_id=sibling,
+            device_id_type=MESH,
+        )
+
     for g in range(2):
-
-        @pl.when(grp == g)
-        def _():
-            whole = pltpu.make_async_remote_copy(
-                src_ref=sent.at[pl.ds(0, HALF - 1 + g), wire],
-                dst_ref=got.at[pl.ds(start, HALF - 1 + g), wire],
-                send_sem=sems.at[0],
-                recv_sem=sems.at[1],
-                device_id=sibling,
-                device_id_type=MESH,
-            )
-            whole.wait_recv()
-            whole.wait_send()
-
+        pl.when(grp == g)(messages(HALF - 1 + g).wait_recv)
     swap = pltpu.make_async_remote_copy(
         src_ref=got.at[pl.ds(start, HALF), wire],
         dst_ref=got.at[pl.ds(start, HALF), wire],
@@ -197,6 +194,8 @@
         device_id_type=MESH,
     )
     swap.start()
+    for g in range(2):
+        pl.when(grp == g)(messages(HALF - 1 + g).wait_send)
     swap.wait()
 
 

time: 44.6 us -> 44.6 us (level)
  no operation moved by 1% of the time
where the time goes in v10:
time: 44.6 us; the launch traced here: 44.4 us
  Pallas kernels  42.1 us (94%)
  local copies, waits for them, and re-layouts  2.25 us (5%)
    pallas_call x1, Pallas kernels, shards(): call(deliver_kernel, 'deliver', 16, jax.ShapeDtypeStruct((CELLS, 8, 128),...  20.4 us
    pallas_call x1, Pallas kernels, shards(): call(receive_kernel, 'receive', 24, jax.ShapeDtypeStruct((USERS, 2, FRAME...  18.6 us
    pallas_call x1, Pallas kernels, shards(): call(transmit_kernel, 'transmit', 24, (jax.ShapeDtypeStruct((CELLS * 8, 1...  3 us
    unnamed x17, local copies, waits for them, and re-layouts  1.31 us
    another operation x1, local copies, waits for them, and re-layouts, shards(): jnp.stack((path_delay, path_angle, path_gain[0], path_gain[1]))  0.94 us

profile of v10, /device:TPU:1, one launch (start us, length us, event | category | flops | bytes accessed | tf_op | source)
XLA Modules:
  0.0 44.4 jit_solution(2306933249890044694)
XLA Ops:
  0.0 0.0 copy-start.6
  0.0 0.0 copy-start.7
  0.0 0.9 %stack.14 = f32[2,65,128]{2,1,0:T(8,128)S(1)} reshape(f32[2,8320]{1,0:T(2,128)} %param.11) | data formatting | bytes 133120 | tf_op jit(solution)/shard_map/stack | solution.py:503
  0.9 0.0 copy-done.6
  1.0 0.0 copy-done.7
  1.0 0.0 copy-start.2
  1.0 0.0 copy-start.3
  1.0 0.0 copy-start.4
  1.0 0.0 copy-start.5
  1.0 0.6 %copy-done.2 = s32[32]{0:T(128)S(1)} copy-done((s32[32]{0:T(128)S(1)}, s32[32]{0:T(128)}, u32[]{:S(2)}) %copy-start.2) | copy-done | bytes 152
  1.6 0.0 copy-done.3
  1.7 0.0 copy-done.4
  1.7 0.0 copy-done.5
  1.7 0.0 copy-start
  1.7 0.0 copy-start.1
  1.7 20.4 %deliver.1.got = f32[128,8,128]{2,1,0:T(8,128)S(1)} custom-call(s32[256]{0:T(256)S(1)} %copy-done.3, s32[256]{0:T(256)S(1)} %copy-done.4, s32[256]{0:T(256)S(1)} %copy-done.5, s32[32]{0:T(128)S(1)} %copy-done.2, f32[4,65,128]{2,1,0:T(8,128)S(1)} %pad_maximum_fusion.fields), custom_call_target="tpu_custom_call" | custom-call | tf_op jit(solution)/shard_map/deliver/pallas_call | solution.py:481
  22.2 0.0 copy-done
  22.2 0.0 copy-done.1
  22.2 3.0 %transmit.1 = (f32[1024,128]{1,0:T(8,128)S(1)}, s32[2,128]{1,0:T(2,128)S(1)}, f32[32,64,128]{2,1,0:T(8,128)S(1)}) custom-call(s32[32]{0:T(128)S(1)} %copy-done.2, s32[8,32]{1,0:T(8,128)S(1)} %copy-done, f32[1024,128]{1,0:T(8,128)S(1)} %bitcast.4, bf16[32,2,128]{2,1,0:T(2,128)(2,1)S(1)} %copy-done.1), custom_call_target="tpu_custom_call" | custom-call | tf_op jit(solution)/shard_map/transmit/pallas_call | solution.py:505
  25.2 18.6 %receive.1 = f32[32,2,128]{2,1,0:T(2,128)S(1)} custom-call(s32[8,32]{1,0:T(8,128)S(1)} %copy-done, s32[2,128]{1,0:T(2,128)S(1)} %get-tuple-element.8.table, f32[128,8,128]{2,1,0:T(8,128)S(1)} %deliver.1.got, f32[128,8,128]{2,1,0:T(8,128)S(1)} %bitcast.5, f32[32,64,128]{2,1,0:T(8,128)S(1)} %get-tuple-element.10.raw), custom_call_target="tpu_custom_call" | custom-call | tf_op jit(solution)/shard_map/receive/pallas_call | solution.py:523
  43.8 0.6 %copy.11 = f32[32,2,128]{2,1,0:T(2,128)} copy(f32[32,2,128]{2,1,0:T(2,128)S(1)} %receive.1) | data formatting | bytes 65536
  (1 shorter events, 0.0 us)
Async XLA Ops:
  0.0 0.9 %copy-start.6 = (f32[8320]{0:T(1024)S(1)}, f32[8320]{0:T(1024)}, u32[]{:S(2)}) copy-start(f32[8320]{0:T(1024)} %param.10) | copy-start | bytes 99844
  0.0 1.0 %copy-start.7 = (f32[8320]{0:T(1024)S(1)}, f32[8320]{0:T(1024)}, u32[]{:S(2)}) copy-start(f32[8320]{0:T(1024)} %param.9) | copy-start | bytes 99844
  1.0 0.7 %copy-start.2 = (s32[32]{0:T(128)S(1)}, s32[32]{0:T(128)}, u32[]{:S(2)}) copy-start(s32[32]{0:T(128)} %slots.1) | copy-start | bytes 388
  1.0 0.7 %copy-start.3 = (s32[256]{0:T(256)S(1)}, s32[256]{0:T(256)}, u32[]{:S(2)}) copy-start(s32[256]{0:T(256)} %counts_in.1) | copy-start | bytes 3076
  1.0 0.7 %copy-start.4 = (s32[256]{0:T(256)S(1)}, s32[256]{0:T(256)}, u32[]{:S(2)}) copy-start(s32[256]{0:T(256)} %offsets_in.1) | copy-start | bytes 3076
  1.0 0.7 %copy-start.5 = (s32[256]{0:T(256)S(1)}, s32[256]{0:T(256)}, u32[]{:S(2)}) copy-start(s32[256]{0:T(256)} %links_in.1) | copy-start | bytes 3076
  1.7 20.5 %copy-start = (s32[8,32]{1,0:T(8,128)S(1)}, s32[8,32]{1,0:T(8,128)}, u32[]{:S(2)}) copy-start(s32[8,32]{1,0:T(8,128)} %nearby.3) | copy-start | bytes 3076
  1.7 20.5 %copy-start.1 = (bf16[32,2,128]{2,1,0:T(2,128)(2,1)S(1)}, bf16[32,2,128]{2,1,0:T(2,128)(2,1)}, u32[]{:S(2)}) copy-start(bf16[32,2,128]{2,1,0:T(2,128)(2,1)} %symbols.1) | copy-start | bytes 49156
